TPU v7x, 32 devices: a whole 2x2x4 slice. The times are simulated.
32 devices in a mesh: dp: 8 (over z, x), tensor: 4 (over y, core).
Axes of the slice: x: 2, y: 2, z: 4, core: 2. Of those that a mesh axis runs over, the one named last changes fastest.
Arguments:
- residual: bfloat16 [8, 1024, 768], P('dp', 'tensor'), may hold values from -64 to 64
- cotangent: bfloat16 [8, 1024, 768], P('dp', 'tensor'), may hold values from -6 to 6
- memory: bfloat16 [8, 2, 2048, 768], P('dp'), may hold values from -6.4 to 6.4
- segment_ids: int32 [8, 1024], P('dp'), may hold values from 0 to 3, as said below
- plot_ids: int32 [8, 4], P('dp'), may hold values from 0 to 1
- attend_weight: float32 [4, 768, 768], P(None, 'dp', 'tensor'), may hold values from -0.2309401 to 0.2309401
- attend_first: float32 [4, 768, 768], P(None, 'dp', 'tensor'), may hold values from -0.00021362305 to 0.00021362305
- attend_second: float32 [4, 768, 768], P(None, 'dp', 'tensor'), may hold values from 1.05937946e-10 to 4.2375178e-10
- recall_weight: float32 [2, 768, 768], P(None, 'dp', 'tensor'), may hold values from -0.2309401 to 0.2309401
- recall_first: float32 [2, 768, 768], P(None, 'dp', 'tensor'), may hold values from -0.00021362305 to 0.00021362305
- recall_second: float32 [2, 768, 768], P(None, 'dp', 'tensor'), may hold values from 1.05937946e-10 to 4.2375178e-10
- outward_weight: float32 [2, 768, 768], P(None, 'tensor', 'dp'), may hold values from -2.6 to 2.6
- outward_first: float32 [2, 768, 768], P(None, 'tensor', 'dp'), may hold values from -0.00021362305 to 0.00021362305
- outward_second: float32 [2, 768, 768], P(None, 'tensor', 'dp'), may hold values from 2.118759e-11 to 8.475036e-11
- expand_weight: float32 [2, 768, 2048], P(None, 'dp', 'tensor'), may hold values from -0.2309401 to 0.2309401
- expand_first: float32 [2, 768, 2048], P(None, 'dp', 'tensor'), may hold values from -0.00021362305 to 0.00021362305
- expand_second: float32 [2, 768, 2048], P(None, 'dp', 'tensor'), may hold values from 2.118759e-11 to 8.475036e-11
- narrow_weight: float32 [2048, 768], P('tensor', 'dp'), may hold values from -0.14142136 to 0.14142136
- narrow_first: float32 [2048, 768], P('tensor', 'dp'), may hold values from -0.00021362305 to 0.00021362305
- narrow_second: float32 [2048, 768], P('tensor', 'dp'), may hold values from 1.05937946e-10 to 4.2375178e-10
- gain_weight: float32 [3, 768], replicated, may hold values from 0.4 to 2.3
- gain_first: float32 [3, 768], replicated, may hold values from -0.00021362305 to 0.00021362305
- gain_second: float32 [3, 768], replicated, may hold values from 1.05937946e-10 to 4.2375178e-10
Outputs:
- block_out: bfloat16 [8, 1024, 768], P('dp', 'tensor')
- residual_grad: bfloat16 [8, 1024, 768], P('dp', 'tensor')
- memory_grad: bfloat16 [8, 2, 2048, 768], P('dp', None, 'tensor')
- grad_norm: float32 [], replicated
- attend_master: float32 [4, 768, 768], P(None, 'dp', 'tensor')
- attend_moment: float32 [4, 768, 768], P(None, 'dp', 'tensor')
- attend_squares: float32 [4, 768, 768], P(None, 'dp', 'tensor')
- attend_copy: bfloat16 [4, 768, 768], P(None, 'dp', 'tensor')
- recall_master: float32 [2, 768, 768], P(None, 'dp', 'tensor')
- recall_moment: float32 [2, 768, 768], P(None, 'dp', 'tensor')
- recall_squares: float32 [2, 768, 768], P(None, 'dp', 'tensor')
- recall_copy: bfloat16 [2, 768, 768], P(None, 'dp', 'tensor')
- outward_master: float32 [2, 768, 768], P(None, 'tensor', 'dp')
- outward_moment: float32 [2, 768, 768], P(None, 'tensor', 'dp')
- outward_squares: float32 [2, 768, 768], P(None, 'tensor', 'dp')
- outward_copy: bfloat16 [2, 768, 768], P(None, 'tensor', 'dp')
- expand_master: float32 [2, 768, 2048], P(None, 'dp', 'tensor')
- expand_moment: float32 [2, 768, 2048], P(None, 'dp', 'tensor')
- expand_squares: float32 [2, 768, 2048], P(None, 'dp', 'tensor')
- expand_copy: bfloat16 [2, 768, 2048], P(None, 'dp', 'tensor')
- narrow_master: float32 [2048, 768], P('tensor', 'dp')
- narrow_moment: float32 [2048, 768], P('tensor', 'dp')
- narrow_squares: float32 [2048, 768], P('tensor', 'dp')
- narrow_copy: bfloat16 [2048, 768], P('tensor', 'dp')
- gain_master: float32 [3, 768], replicated
- gain_moment: float32 [3, 768], replicated
- gain_squares: float32 [3, 768], replicated
Inputs may be any that keep to these rules, and one draw needn't show every extreme that they name: `segment_ids`: in every row the ids never fall, and every id holds one token or more.
All inputs are finite; a program needn't handle non-finite values.
Results may differ from a plain program's by a relative error of at most 0.03.
The roundings to bfloat16 on the way count: a program that leaves them out, or rounds other values in their place, can miss the bound.
Values may be sent and summed in bfloat16 or wider, within the bound.
A program may use at most 320 MiB of HBM per device.

v0:
```python
import jax
import jax.numpy as jnp
from jax import lax
from jax.sharding import PartitionSpec as P

HEAD = 64
PATCHES = 2048
SEGS = 4
STEP = 10


NORM_EPS = 1e-06
ADAM_EPS = 1e-08
BETA_ONE = 0.9
BETA_TWO = 0.999
DECAY = 0.1
RATE_INNER = 0.05
RATE_OUTER = 0.4
RATE_GAIN = 0.5
CLIP = 1.0
MASKED = -1e30


def normalize(stream, gain):
    scale_rows = lax.rsqrt(jnp.mean(stream * stream, axis=-1, keepdims=True) + NORM_EPS)
    return stream * scale_rows * gain


def norm_back(stream, gain, grad_normed):
    unused, pullback = jax.vjp(normalize, stream, gain)
    return pullback(grad_normed)


def spread_rows(stream, gain):
    normed = normalize(stream, gain).astype(jnp.bfloat16)
    return lax.all_gather(normed, "tensor", axis=1, tiled=True)


def collect_grads(grad_stream):
    return lax.all_gather(grad_stream.astype(jnp.bfloat16), "tensor", axis=1, tiled=True)


def sum_branch(partial_out):
    return lax.psum_scatter(partial_out, "tensor", scatter_dimension=1, tiled=True)


def sum_inputs(partial_grad):
    return lax.psum_scatter(partial_grad, "tensor", scatter_dimension=1, tiled=True)


def project(left, right):
    return jnp.einsum("...k,kn->...n", left, right, preferred_element_type=jnp.float32)


def project_back(left, right):
    return jnp.einsum("...n,kn->...k", left, right, preferred_element_type=jnp.float32)


def outer_total(left, right):
    return jnp.einsum("rlk,rln->kn", left, right, preferred_element_type=jnp.float32)


def split_heads(values):
    return values.reshape(values.shape[0], values.shape[1], -1, HEAD)


def merge_heads(values):
    return values.reshape(values.shape[0], values.shape[1], -1)


def activate(gate_value, lifted):
    return jax.nn.gelu(gate_value, approximate=True) * lifted


def causal_permit(segments):
    places = jnp.arange(segments.shape[1])

    def permit(row_start, block_rows):
        query_segments = segments[:, row_start : row_start + block_rows]
        matching = query_segments[:, :, None] == segments[:, None, :]
        earlier = places[None, :] <= places[row_start : row_start + block_rows][:, None]
        return matching & earlier[None]

    return permit


def plot_permit(token_plots, key_total):
    key_plots = jnp.arange(key_total) // PATCHES

    def permit(row_start, block_rows):
        return token_plots[:, row_start : row_start + block_rows, None] == key_plots[None, None, :]

    return permit


def block_scores(query_block, keys_all, allowed):
    scores = jnp.einsum(
        "rqhd,rkhd->rhqk", query_block, keys_all, preferred_element_type=jnp.float32
    ) * HEAD ** (-0.5)
    return jnp.where(allowed[:, None], scores, MASKED)


def attend_forward(queries, keys_all, values_all, permit):
    length = queries.shape[1]
    block_rows = min(512, length)
    mixture_parts = []
    log_parts = []
    for row_start in range(0, length, block_rows):
        scores = block_scores(
            queries[:, row_start : row_start + block_rows], keys_all, permit(row_start, block_rows)
        )
        row_peak = jnp.max(scores, axis=-1, keepdims=True)
        raised = jnp.exp(scores - row_peak)
        row_total = jnp.sum(raised, axis=-1, keepdims=True)
        weights = (raised / row_total).astype(jnp.bfloat16)
        mixture_parts.append(
            jnp.einsum("rhqk,rkhd->rqhd", weights, values_all, preferred_element_type=jnp.float32)
        )
        log_parts.append(row_peak + jnp.log(row_total))
    return (jnp.concatenate(mixture_parts, axis=1), jnp.concatenate(log_parts, axis=2))


def attend_backward(queries, keys_all, values_all, log_totals, grad_mixture, permit):
    length = queries.shape[1]
    block_rows = min(512, length)
    score_scale = HEAD ** (-0.5)
    mixture_parts = []
    query_parts = []
    key_grad = jnp.zeros(keys_all.shape, jnp.float32)
    value_grad = jnp.zeros(values_all.shape, jnp.float32)
    for row_start in range(0, length, block_rows):
        query_block = queries[:, row_start : row_start + block_rows]
        grad_block = grad_mixture[:, row_start : row_start + block_rows]
        scores = block_scores(query_block, keys_all, permit(row_start, block_rows))
        probabilities = jnp.exp(scores - log_totals[:, :, row_start : row_start + block_rows])
        weights = probabilities.astype(jnp.bfloat16)
        mixture_parts.append(
            jnp.einsum("rhqk,rkhd->rqhd", weights, values_all, preferred_element_type=jnp.float32)
        )
        value_grad = value_grad + jnp.einsum(
            "rhqk,rqhd->rkhd", weights, grad_block, preferred_element_type=jnp.float32
        )
        prob_grad = jnp.einsum(
            "rqhd,rkhd->rhqk", grad_block, values_all, preferred_element_type=jnp.float32
        )
        inner_sum = jnp.sum(probabilities * prob_grad, axis=-1, keepdims=True)
        score_grad = (probabilities * (prob_grad - inner_sum)).astype(jnp.bfloat16)
        query_parts.append(
            jnp.einsum("rhqk,rkhd->rqhd", score_grad, keys_all, preferred_element_type=jnp.float32)
            * score_scale
        )
        key_grad = (
            key_grad
            + jnp.einsum(
                "rhqk,rqhd->rkhd", score_grad, query_block, preferred_element_type=jnp.float32
            )
            * score_scale
        )
    return (
        jnp.concatenate(mixture_parts, axis=1),
        jnp.concatenate(query_parts, axis=1),
        key_grad,
        value_grad,
    )


def adam_step(master, moment, second, gradient, step_rate, decay_rate):
    moment_new = BETA_ONE * moment + (1.0 - BETA_ONE) * gradient
    second_new = BETA_TWO * second + (1.0 - BETA_TWO) * gradient * gradient
    moment_hat = moment_new / (1.0 - BETA_ONE**STEP)
    second_hat = second_new / (1.0 - BETA_TWO**STEP)
    master_new = master - step_rate * (
        moment_hat / (jnp.sqrt(second_hat) + ADAM_EPS) + decay_rate * master
    )
    return (master_new, moment_new, second_new)


def local(
    residual,
    cotangent,
    memory,
    segment_ids,
    plot_ids,
    attend_weight,
    attend_first,
    attend_second,
    recall_weight,
    recall_first,
    recall_second,
    outward_weight,
    outward_first,
    outward_second,
    expand_weight,
    expand_first,
    expand_second,
    narrow_weight,
    narrow_first,
    narrow_second,
    gain_weight,
    gain_first,
    gain_second,
):
    attend_full, recall_full, outward_full, expand_full, narrow_full = (
        lax.all_gather(attend_weight.astype(jnp.bfloat16), "dp", axis=1, tiled=True),
        lax.all_gather(recall_weight.astype(jnp.bfloat16), "dp", axis=1, tiled=True),
        lax.all_gather(outward_weight.astype(jnp.bfloat16), "dp", axis=2, tiled=True),
        lax.all_gather(expand_weight.astype(jnp.bfloat16), "dp", axis=1, tiled=True),
        lax.all_gather(narrow_weight.astype(jnp.bfloat16), "dp", axis=1, tiled=True),
    )
    rows_count = memory.shape[0]
    plot_count = memory.shape[1]
    patch_count = memory.shape[2]
    feature_count = memory.shape[3]
    memory_flat = memory.reshape(rows_count, plot_count * patch_count, feature_count)
    token_plots = jnp.sum(
        jnp.where(
            segment_ids[:, :, None] == jnp.arange(SEGS)[None, None, :], plot_ids[:, None, :], 0
        ),
        axis=-1,
    )
    self_permit = causal_permit(segment_ids)
    cross_permit = plot_permit(token_plots, plot_count * patch_count)

    def self_inputs(rows_in):
        queries = split_heads(project(rows_in, attend_full[0]).astype(jnp.bfloat16))
        keys_self = split_heads(project(rows_in, attend_full[1]).astype(jnp.bfloat16))
        values_self = split_heads(project(rows_in, attend_full[2]).astype(jnp.bfloat16))
        return (queries, keys_self, values_self)

    def cross_inputs(rows_in):
        queries = split_heads(project(rows_in, attend_full[3]).astype(jnp.bfloat16))
        keys_cross = split_heads(project(memory_flat, recall_full[0]).astype(jnp.bfloat16))
        values_cross = split_heads(project(memory_flat, recall_full[1]).astype(jnp.bfloat16))
        return (queries, keys_cross, values_cross)

    stream_zero = residual.astype(jnp.float32)
    rows_zero = spread_rows(stream_zero, gain_weight[0])
    queries, keys_self, values_self = self_inputs(rows_zero)
    mixture, totals_self = attend_forward(queries, keys_self, values_self, self_permit)
    stream_one = stream_zero + sum_branch(
        project(merge_heads(mixture).astype(jnp.bfloat16), outward_full[0])
    )
    rows_one = spread_rows(stream_one, gain_weight[1])
    queries, keys_cross, values_cross = cross_inputs(rows_one)
    mixture, totals_cross = attend_forward(queries, keys_cross, values_cross, cross_permit)
    stream_two = stream_one + sum_branch(
        project(merge_heads(mixture).astype(jnp.bfloat16), outward_full[1])
    )
    rows_two = spread_rows(stream_two, gain_weight[2])
    activated = activate(
        project(rows_two, expand_full[0]), project(rows_two, expand_full[1])
    ).astype(jnp.bfloat16)
    block_out = stream_two + sum_branch(project(activated, narrow_full))
    grad_stream = cotangent.astype(jnp.float32)
    rows_again = spread_rows(stream_two, gain_weight[2])
    grad_rows = collect_grads(grad_stream)
    activated_full, activate_pull = jax.vjp(
        activate, project(rows_again, expand_full[0]), project(rows_again, expand_full[1])
    )
    grad_narrow = outer_total(activated_full.astype(jnp.bfloat16), grad_rows)
    grad_gate, grad_lifted = activate_pull(project_back(grad_rows, narrow_full))
    grad_gate = grad_gate.astype(jnp.bfloat16)
    grad_lifted = grad_lifted.astype(jnp.bfloat16)
    grad_expand = jnp.stack(
        [outer_total(rows_again, grad_gate), outer_total(rows_again, grad_lifted)]
    )
    grad_normed = sum_inputs(
        project_back(grad_gate, expand_full[0]) + project_back(grad_lifted, expand_full[1])
    )
    grad_part, gain_grad_two = norm_back(stream_two, gain_weight[2], grad_normed)
    grad_stream = grad_stream + grad_part
    rows_again = spread_rows(stream_one, gain_weight[1])
    grad_rows = collect_grads(grad_stream)
    queries, keys_cross, values_cross = cross_inputs(rows_again)
    grad_mixture = split_heads(project_back(grad_rows, outward_full[1]).astype(jnp.bfloat16))
    mixture, grad_query, grad_key, grad_value = attend_backward(
        queries, keys_cross, values_cross, totals_cross, grad_mixture, cross_permit
    )
    grad_out_cross = outer_total(merge_heads(mixture).astype(jnp.bfloat16), grad_rows)
    grad_query = merge_heads(grad_query).astype(jnp.bfloat16)
    grad_key = merge_heads(grad_key).astype(jnp.bfloat16)
    grad_value = merge_heads(grad_value).astype(jnp.bfloat16)
    grad_attend_cross = outer_total(rows_again, grad_query)
    grad_recall = jnp.stack(
        [outer_total(memory_flat, grad_key), outer_total(memory_flat, grad_value)]
    )
    query_part = project_back(grad_query, attend_full[3])
    memory_part = project_back(grad_key, recall_full[0]) + project_back(grad_value, recall_full[1])
    grad_normed, memory_grad = (
        lax.psum_scatter(
            query_part.astype(jnp.bfloat16), "tensor", scatter_dimension=1, tiled=True
        ).astype(jnp.float32),
        lax.psum_scatter(
            memory_part.reshape(rows_count, plot_count, patch_count, feature_count).astype(
                jnp.bfloat16
            ),
            "tensor",
            scatter_dimension=2,
            tiled=True,
        ).astype(jnp.float32),
    )
    grad_part, gain_grad_one = norm_back(stream_one, gain_weight[1], grad_normed)
    grad_stream = grad_stream + grad_part
    rows_again = spread_rows(stream_zero, gain_weight[0])
    grad_rows = collect_grads(grad_stream)
    queries, keys_self, values_self = self_inputs(rows_again)
    grad_mixture = split_heads(project_back(grad_rows, outward_full[0]).astype(jnp.bfloat16))
    mixture, grad_query, grad_key, grad_value = attend_backward(
        queries, keys_self, values_self, totals_self, grad_mixture, self_permit
    )
    grad_out_self = outer_total(merge_heads(mixture).astype(jnp.bfloat16), grad_rows)
    grad_query = merge_heads(grad_query).astype(jnp.bfloat16)
    grad_key = merge_heads(grad_key).astype(jnp.bfloat16)
    grad_value = merge_heads(grad_value).astype(jnp.bfloat16)
    grad_attend = jnp.stack(
        [
            outer_total(rows_again, grad_query),
            outer_total(rows_again, grad_key),
            outer_total(rows_again, grad_value),
            grad_attend_cross,
        ]
    )
    grad_normed = sum_inputs(
        project_back(grad_query, attend_full[0])
        + project_back(grad_key, attend_full[1])
        + project_back(grad_value, attend_full[2])
    )
    grad_part, gain_grad_zero = norm_back(stream_zero, gain_weight[0], grad_normed)
    residual_grad = grad_stream + grad_part
    grad_outward = jnp.stack([grad_out_self, grad_out_cross])
    owned_grads = (
        lax.psum_scatter(grad_attend, "dp", scatter_dimension=1, tiled=True),
        lax.psum_scatter(grad_recall, "dp", scatter_dimension=1, tiled=True),
        lax.psum_scatter(grad_outward, "dp", scatter_dimension=2, tiled=True),
        lax.psum_scatter(grad_expand, "dp", scatter_dimension=1, tiled=True),
        lax.psum_scatter(grad_narrow, "dp", scatter_dimension=1, tiled=True),
    )
    gain_grads = jnp.stack([gain_grad_zero, gain_grad_one, gain_grad_two])
    local_squares = sum((jnp.sum(owned_piece * owned_piece) for owned_piece in owned_grads))
    gain_total, square_total = lax.psum((gain_grads, local_squares), ("dp", "tensor"))
    grad_norm = jnp.sqrt(square_total + jnp.sum(gain_total * gain_total))
    factor = jnp.minimum(1.0, CLIP / (grad_norm + 1e-06))
    masters = (attend_weight, recall_weight, outward_weight, expand_weight, narrow_weight)
    moments = (attend_first, recall_first, outward_first, expand_first, narrow_first)
    seconds = (attend_second, recall_second, outward_second, expand_second, narrow_second)
    step_rates = (RATE_INNER, RATE_INNER, RATE_OUTER, RATE_INNER, RATE_INNER)
    results = []
    for master, moment, second, gradient, step_rate in zip(
        masters, moments, seconds, owned_grads, step_rates
    ):
        master_new, moment_new, second_new = adam_step(
            master, moment, second, gradient * factor, step_rate, DECAY
        )
        results.extend([master_new, moment_new, second_new, master_new.astype(jnp.bfloat16)])
    gain_new = adam_step(gain_weight, gain_first, gain_second, gain_total * factor, RATE_GAIN, 0.0)
    return (
        (
            block_out.astype(jnp.bfloat16),
            residual_grad.astype(jnp.bfloat16),
            memory_grad.astype(jnp.bfloat16),
            grad_norm,
        )
        + tuple(results)
        + tuple(gain_new)
    )


def solution(mesh):
    in_specs = (
        P("dp", "tensor", None),
        P("dp", "tensor", None),
        P("dp", None, None, None),
        P("dp", None),
        P("dp", None),
        P(None, "dp", "tensor"),
        P(None, "dp", "tensor"),
        P(None, "dp", "tensor"),
        P(None, "dp", "tensor"),
        P(None, "dp", "tensor"),
        P(None, "dp", "tensor"),
        P(None, "tensor", "dp"),
        P(None, "tensor", "dp"),
        P(None, "tensor", "dp"),
        P(None, "dp", "tensor"),
        P(None, "dp", "tensor"),
        P(None, "dp", "tensor"),
        P("tensor", "dp"),
        P("tensor", "dp"),
        P("tensor", "dp"),
        P(),
        P(),
        P(),
    )
    out_specs = (
        P("dp", "tensor", None),
        P("dp", "tensor", None),
        P("dp", None, "tensor", None),
        P(),
        P(None, "dp", "tensor"),
        P(None, "dp", "tensor"),
        P(None, "dp", "tensor"),
        P(None, "dp", "tensor"),
        P(None, "dp", "tensor"),
        P(None, "dp", "tensor"),
        P(None, "dp", "tensor"),
        P(None, "dp", "tensor"),
        P(None, "tensor", "dp"),
        P(None, "tensor", "dp"),
        P(None, "tensor", "dp"),
        P(None, "tensor", "dp"),
        P(None, "dp", "tensor"),
        P(None, "dp", "tensor"),
        P(None, "dp", "tensor"),
        P(None, "dp", "tensor"),
        P("tensor", "dp"),
        P("tensor", "dp"),
        P("tensor", "dp"),
        P("tensor", "dp"),
        P(),
        P(),
        P(),
    )
    return jax.shard_map(local, mesh=mesh, in_specs=in_specs, out_specs=out_specs, check_vma=False)
```

profile of v0, /device:TPU:0, one launch (start us, length us, event | category | flops | bytes accessed | tf_op | source)
XLA Modules:
  0.0 1108.2 jit_solution(11893417375158420728)
XLA Ops:
  15.8 35.3 %all_gather.38 = bf16[2,192,768]{1,0,2:T(2,128)(2,1)S(1)} all-gather(bf16[2,192,96]{1,0,2:T(2,128)(2,1)S(1)} %copy.102), channel_id=1, replica_groups=mesh['dp'=8,'tensor'=4] {'dp'}, dimensions={2}, use_global_device_ids=true | all-gather | bytes 663552 | tf_op jit(solution)/shard_map/all_gather | solution.py:206
  54.0 7.6 all-gather.11.cloned.1.call-done
  61.5 21.5 %all-gather.9.cloned.1.call-done = bf16[1,1024,768]{2,1,0:T(8,128)(2,1)} async-done(((bf16[1,256,768]{2,1,0:T(8,128)(2,1)}), bf16[1,1024,768]{2,1,0:T(8,128)(2,1)}) %all-gather.9.cloned.1.call-update) | async-done | bytes 1572880 | tf_op jit(solution)/shard_map/all_gather | solution.py:36
  85.1 2.3 fusion.101
  102.5 37.8 %reduce-scatter.19.cloned.1.call-done = f32[1,256,768]{2,1,0:T(8,128)} async-done(((f32[1,1024,768]{2,1,0:T(8,128)}), f32[1,256,768]{2,1,0:T(8,128)}) %reduce-scatter.19.cloned.1.call-update) | async-done | bytes 786448 | tf_op jit(solution)/shard_map/reduce_scatter | solution.py:44
  144.0 32.2 %all_gather.39 = bf16[2,768,192]{2,1,0:T(8,128)(2,1)S(1)} all-gather(bf16[2,96,192]{2,1,0:T(8,128)(2,1)S(1)} %convert_element_type.314), channel_id=1, replica_groups=mesh['dp'=8,'tensor'=4] {'dp'}, dimensions={1}, use_global_device_ids=true | all-gather | bytes 663552 | tf_op jit(solution)/shard_map/all_gather | solution.py:205
  176.2 6.5 convolution_convert_fusion
  182.7 3.4 convolution_convert_fusion.1
  186.1 4.2 broadcast_compare_fusion.1
  192.4 12.5 %fusion.211 = (f32[3,512]{1,0:T(4,128)S(1)}, f32[3,512,4096]{2,1,0:T(8,128)}) fusion(bf16[4096,3,64]{0,2,1:T(8,128)(2,1)S(1)} %bitcast.377, bf16[1,1024,3,64]{1,3,2,0:T(8,128)(2,1)S(1)} %bitcast.393, pred[512,4096]{1,0:T(8,128)(4,1)} %get-tuple-element.182), kind=kOutput, calls=%fused_computation.301 | convolution fusion | flops 824179200 | bytes 29038592 | tf_op jit(solution)/shard_map/rqhd,rkhd->rhqk/dot_general | solution.py:97
  204.9 11.0 fusion.212
  215.9 10.6 fusion.1
  226.5 10.6 fusion.125
  237.1 10.5 fusion
  247.6 11.0 fusion.126
  258.6 2.4 convolution_bitcast_fusion.1
  261.8 37.3 %reduce-scatter.21.cloned.1.call-done = f32[1,256,768]{2,1,0:T(8,128)} async-done(((f32[1,1024,768]{2,1,0:T(8,128)}), f32[1,256,768]{2,1,0:T(8,128)}) %reduce-scatter.21.cloned.1.call-update) | async-done | bytes 786448 | tf_op jit(solution)/shard_map/reduce_scatter | solution.py:44
  303.0 33.0 %all_gather.43 = bf16[512,768]{0,1:T(8,128)(2,1)S(1)} all-gather(bf16[512,96]{0,1:T(8,128)(2,1)S(1)} %convert_element_type.324), channel_id=1, replica_groups=mesh['dp'=8,'tensor'=4] {'dp'}, dimensions={1}, use_global_device_ids=true | all-gather | bytes 884736 | tf_op jit(solution)/shard_map/all_gather | solution.py:208
  336.0 11.9 %all-gather.17.cloned.1.call-done = bf16[2,768,512]{2,1,0:T(8,128)(2,1)} async-done(((bf16[2,96,512]{2,1,0:T(8,128)(2,1)}), bf16[2,768,512]{2,1,0:T(8,128)(2,1)}) %all-gather.17.cloned.1.call-update) | async-done | bytes 1572880 | tf_op jit(solution)/shard_map/all_gather | solution.py:207
  347.9 21.2 %all-gather.15.cloned.1.call-done = bf16[1,1024,768]{2,1,0:T(8,128)(2,1)} async-done(((bf16[1,256,768]{2,1,0:T(8,128)(2,1)}), bf16[1,1024,768]{2,1,0:T(8,128)(2,1)}) %all-gather.15.cloned.1.call-update) | async-done | bytes 1572880 | tf_op jit(solution)/shard_map/all_gather | solution.py:36
  369.1 4.1 fusion.47
  375.4 14.9 %all-gather.19.cloned.1.call-done = bf16[1,1024,768]{2,1,0:T(8,128)(2,1)} async-done(((bf16[1,256,768]{2,1,0:T(8,128)(2,1)}), bf16[1,1024,768]{2,1,0:T(8,128)(2,1)}) %all-gather.19.cloned.1.call-update) | async-done | bytes 1572880 | tf_op jit(solution)/shard_map/all_gather | solution.py:40
  390.4 5.3 multiply_convert_fusion.4
  397.0 2.7 add_bitcast_fusion.1
  399.9 38.1 %reduce-scatter.25.cloned.1.call-done = f32[1,256,768]{2,1,0:T(8,128)} async-done(((f32[1,1024,768]{2,1,0:T(8,128)}), f32[1,256,768]{2,1,0:T(8,128)}) %reduce-scatter.25.cloned.1.call-update) | async-done | bytes 786448 | tf_op jit(solution)/shard_map/reduce_scatter | solution.py:48
  442.1 19.7 %all-gather.21.cloned.1.call-done = bf16[1,1024,768]{2,1,0:T(8,128)(2,1)} async-done(((bf16[1,256,768]{2,1,0:T(8,128)(2,1)}), bf16[1,1024,768]{2,1,0:T(8,128)(2,1)}) %all-gather.21.cloned.1.call-update) | async-done | bytes 1572880 | tf_op jit(solution)/shard_map/all_gather | solution.py:40
  463.9 19.6 %multiply_reduce_fusion = (f32[3,512]{1,0:T(4,128)S(1)}, f32[3,512,4096]{2,1,0:T(8,128)}) fusion(f32[3,512,4096]{2,1,0:T(8,128)} %get-tuple-element.194, f32[3,512]{1,0:T(4,128)S(1)} %log_add_fusion.2, bf16[4096,3,64]{0,2,1:T(8,128)(2,1)S(1)} %bitcast.371, bf16[1,1024,3,64]{1,3,2,0:T(8,128)(2,1)S(1)} %bitcast.413), kind=kOutput, calls=%fused_computation.1 | convolution fusion | flops 824179200 | bytes 52115456 | tf_op jit(solution)/shard_map/rqhd,rkhd->rhqk/dot_general | solution.py:143
  483.5 16.9 %multiply_convert_fusion = bf16[3,512,4096]{2,1,0:T(8,128)(2,1)S(1)} fusion(f32[3,512,4096]{2,1,0:T(8,128)} %get-tuple-element.198, f32[3,512,4096]{2,1,0:T(8,128)} %get-tuple-element.194, f32[3,512]{1,0:T(4,128)S(1)} %get-tuple-element.197, f32[3,512]{1,0:T(4,128)S(1)} %log_add_fusion.2), kind=kLoop, calls=%fused_computation | loop fusion | flops 25165824 | bytes 62926848 | tf_op jit(solution)/shard_map/convert_element_type | solution.py:147
  500.4 4.5 copy-done.3
  504.9 6.0 fusion.114
  511.0 15.7 %multiply_reduce_fusion.1 = (f32[3,512]{1,0:T(4,128)S(1)}, f32[3,512,4096]{2,1,0:T(8,128)}) fusion(f32[3,512,4096]{2,1,0:T(8,128)} %get-tuple-element.196, f32[3,512]{1,0:T(4,128)S(1)} %log_add_fusion.3, bf16[4096,3,64]{0,2,1:T(8,128)(2,1)S(1)} %bitcast.372, bf16[1,1024,3,64]{1,3,2,0:T(8,128)(2,1)} %bitcast.414), kind=kOutput, calls=%fused_computation.4 | convolution fusion | flops 824179200 | bytes 52113408 | tf_op jit(solution)/shard_map/rqhd,rkhd->rhqk/dot_general | solution.py:143
  526.7 17.3 %multiply_convert_fusion.1 = bf16[3,512,4096]{2,1,0:T(8,128)(2,1)S(1)} fusion(f32[3,512,4096]{2,1,0:T(8,128)} %get-tuple-element.200, f32[3,512,4096]{2,1,0:T(8,128)} %get-tuple-element.196, f32[3,512]{1,0:T(4,128)S(1)} %get-tuple-element.199, f32[3,512]{1,0:T(4,128)S(1)} %log_add_fusion.3), kind=kLoop, calls=%fused_computation.3 | loop fusion | flops 25165824 | bytes 62926848 | tf_op jit(solution)/shard_map/convert_element_type | solution.py:147
  543.9 7.2 fusion.113
  551.1 3.0 fusion.73
  554.2 4.2 convolution_bitcast_fusion
  558.5 24.0 %reduce-scatter.27.cloned.1.call-done = bf16[1,256,768]{2,1,0:T(8,128)(2,1)} async-done(((bf16[1,1024,768]{2,1,0:T(8,128)(2,1)}), bf16[1,256,768]{2,1,0:T(8,128)(2,1)}) %reduce-scatter.27.cloned.1.call-update) | async-done | bytes 393232 | tf_op jit(solution)/shard_map/reduce_scatter | solution.py:290
  583.7 39.1 %reduce-scatter.23.cloned.1.call-done = f32[1,256,768]{2,1,0:T(8,128)} async-done(((f32[1,1024,768]{2,1,0:T(8,128)}), f32[1,256,768]{2,1,0:T(8,128)}) %reduce-scatter.23.cloned.1.call-update) | async-done | bytes 786448 | tf_op jit(solution)/shard_map/reduce_scatter | solution.py:44
  622.8 3.3 fusion.204
  626.2 4.0 fusion.39
  630.4 4.8 convolution_convert_fusion.4
  635.2 4.6 convolution_convert_fusion.3
  639.8 11.1 %fusion.122 = bf16[3,64,512]{2,1,0:T(8,128)(2,1)} fusion(bf16[4096,3,64]{0,2,1:T(8,128)(2,1)S(1)} %bitcast.373, f32[3,512,4096]{2,1,0:T(8,128)} %get-tuple-element.194, f32[3,512]{1,0:T(4,128)S(1)} %log_add_fusion.2), kind=kOutput, calls=%fused_computation.154 | convolution fusion | flops 817987584 | bytes 26941440 | tf_op jit(solution)/shard_map/rhqk,rkhd->rqhd/dot_general | solution.py:138
  651.0 2.6 fusion.70
  656.6 11.0 fusion.119
  667.6 10.9 fusion.18
  678.6 13.8 %fusion.9 = bf16[3,64,4096]{2,1,0:T(8,128)(2,1)} fusion(f32[3,64,4096]{2,1,0:T(8,128)S(1)} %fusion.18, f32[3,512,4096]{2,1,0:T(8,128)} %get-tuple-element.194, f32[3,512]{1,0:T(4,128)S(1)} %log_add_fusion.2, bf16[1,1024,3,64]{1,3,2,0:T(8,128)(2,1)} %bitcast.416), kind=kOutput, calls=%fused_computation.36 | convolution fusion | flops 819462144 | bytes 30087168 | tf_op jit(solution)/shard_map/rhqk,rqhd->rkhd/dot_general | solution.py:140
  692.4 3.0 convolution_bitcast_fusion.3
  695.4 7.0 fusion.172
  702.5 2.3 fusion.10
  708.5 3.3 reshape.1170
  722.6 4.2 multiply_reduce_fusion.2
  731.8 3.6 multiply_reduce_fusion.3
  735.6 5.7 multiply_convert_fusion.3
  751.3 3.1 copy.121
  754.4 3.2 reshape.1168
  760.6 2.4 add_bitcast_fusion
  764.4 3.0 fusion.163
  767.4 4.6 add_convert_fusion
  775.5 15.6 %reduce-scatter.33.cloned.1.call-done = f32[2,96,512]{2,1,0:T(8,128)} async-done(((f32[2,768,512]{2,1,0:T(8,128)}), f32[2,96,512]{2,1,0:T(8,128)}) %reduce-scatter.33.cloned.1.call-update) | async-done | bytes 393232 | tf_op jit(solution)/shard_map/reduce_scatter | solution.py:335
  792.8 64.7 %reduce-scatter.39.cloned.1.call-done = f32[96,384]{1,0:T(8,128)} async-done(((f32[768,384]{1,0:T(8,128)}), f32[96,384]{1,0:T(8,128)}) %reduce-scatter.39.cloned.1.call-update) | async-done | bytes 147472
  860.0 63.9 %reduce-scatter.41.cloned.1.call-done = f32[96,384]{1,0:T(8,128)} async-done(((f32[768,384]{1,0:T(8,128)}), f32[96,384]{1,0:T(8,128)}) %reduce-scatter.41.cloned.1.call-update) | async-done | bytes 147472
  925.8 69.5 %reduce-scatter.37.cloned.1.call-done = f32[96,768]{1,0:T(8,128)} async-done(((f32[768,768]{1,0:T(8,128)}), f32[96,768]{1,0:T(8,128)}) %reduce-scatter.37.cloned.1.call-update) | async-done | bytes 294928
  1000.7 34.1 %reduce-scatter.29.cloned.1.call-done = f32[1,256,768]{2,1,0:T(8,128)} async-done(((f32[1,1024,768]{2,1,0:T(8,128)}), f32[1,256,768]{2,1,0:T(8,128)}) %reduce-scatter.29.cloned.1.call-update) | async-done | bytes 786448 | tf_op jit(solution)/shard_map/reduce_scatter | solution.py:48
  1037.0 39.8 %all-reduce = (f32[]{:T(128)}, f32[3,768]{1,0:T(4,128)S(1)}) all-reduce(f32[]{:T(128)S(6)} %add.311, f32[3,768]{1,0:T(4,128)S(1)} %pad_maximum_fusion.10), channel_id=1, replica_groups=mesh['dp'=8,'tensor'=4] {'dp','tensor'}, use_global_device_ids=true, to_apply=%region_36.37 | all-reduce | flops 2305 | bytes 18440 | tf_op jit(solution)/shard_map/psum | solution.py:340
  (389 shorter events, 122.2 us)
Async XLA Ops:
  7.2 54.3 %all-gather.11.cloned.1.call-start = ((), (), s32[]{:S(2)}) async-start(), calls=%async_computation.13 | async-start | bytes 1769472 | tf_op jit(solution)/shard_map/all_gather | solution.py:204
  9.0 74.0 %all-gather.9.cloned.1.call-start = ((), (), s32[]{:S(2)}) async-start(), calls=%async_computation.12 | async-start | bytes 1966080 | tf_op jit(solution)/shard_map/all_gather | solution.py:36
  10.5 131.2 %copy-start.79 = (f32[768]{0:T(1024)}, f32[768]{0:T(1024)S(1)}, u32[]{:S(2)}) copy-start(f32[768]{0:T(1024)S(1)} %get-tuple-element.142) | copy-start | bytes 9220
  12.7 40.0 %copy-start.81 = (s32[1,1024]{1,0:T(1,128)S(1)}, s32[1,1024]{1,0:T(1,128)}, u32[]{:S(2)}) copy-start(s32[1,1024]{1,0:T(1,128)} %param.26) | copy-start | bytes 12292
  14.6 125.6 %reduce-scatter.19.cloned.1.call-start = ((), (), s32[]{:S(2)}) async-start(), calls=%async_computation.14 | async-start | bytes 3932160 | tf_op jit(solution)/shard_map/reduce_scatter | solution.py:44
  52.7 47.1 %copy-start.51 = (bf16[1,192,768]{2,1,0:T(8,128)(2,1)}, bf16[1,192,768]{2,1,0:T(8,128)(2,1)S(1)}, u32[]{:S(2)}) copy-start(bf16[1,192,768]{2,1,0:T(8,128)(2,1)S(1)} %copy.127) | copy-start | bytes 884740
  99.8 40.4 %copy-start.21 = (bf16[1,256,768]{2,1,0:T(8,128)(2,1)S(1)}, bf16[1,256,768]{2,1,0:T(8,128)(2,1)}, u32[]{:S(2)}) copy-start(bf16[1,256,768]{2,1,0:T(8,128)(2,1)} %param.23) | copy-start | bytes 1179652
  102.1 41.3 %copy-start.60 = (f32[2,96,192]{2,1,0:T(8,128)S(1)}, f32[2,96,192]{2,1,0:T(8,128)}, u32[]{:S(2)}) copy-start(f32[2,96,192]{2,1,0:T(8,128)} %param.31) | copy-start | bytes 442372
  102.1 88.1 %all-gather.13.cloned.1.call-start = ((), (), s32[]{:S(2)}) async-start(), calls=%async_computation.15 | async-start | bytes 1966080 | tf_op jit(solution)/shard_map/all_gather | solution.py:36
  143.4 155.7 %reduce-scatter.21.cloned.1.call-start = ((), (), s32[]{:S(2)}) async-start(), calls=%async_computation.16 | async-start | bytes 3932160 | tf_op jit(solution)/shard_map/reduce_scatter | solution.py:44
  143.5 39.2 %slice-start.11 = ((s8[6291456]{0:T(1024)(128)(4,1)}), s8[2097152]{0:T(1024)(128)(4,1)S(1)}, s32[]{:S(2)}) async-start(s8[6291456]{0:T(1024)(128)(4,1)} %bitcast.362), calls=%async_computation.43 | async-start | bytes 4194304
  144.0 114.5 %copy-start.52 = (bf16[1,192,768]{2,1,0:T(8,128)(2,1)}, bf16[1,192,768]{2,1,0:T(8,128)(2,1)S(1)}, u32[]{:S(2)}) copy-start(bf16[1,192,768]{2,1,0:T(8,128)(2,1)S(1)} %copy.128) | copy-start | bytes 884740
  192.4 12.5 %copy-start.23 = (bf16[1024,192]{0,1:T(8,128)(2,1)}, bf16[1024,192]{0,1:T(8,128)(2,1)S(1)}, u32[]{:S(2)}) copy-start(bf16[1024,192]{0,1:T(8,128)(2,1)S(1)} %fusion.104) | copy-start | bytes 1179652
  192.4 12.5 %copy-start.42 = (pred[512,4096]{1,0:T(8,128)(4,1)S(1)}, pred[512,4096]{1,0:T(8,128)(4,1)}, u32[]{:S(2)}) copy-start(pred[512,4096]{1,0:T(8,128)(4,1)} %get-tuple-element.181) | copy-start | bytes 6291460
  215.9 10.6 copy-start.6
  258.5 40.5 %copy-start.13 = (f32[1,256,768]{2,1,0:T(8,128)S(1)}, f32[1,256,768]{2,1,0:T(8,128)}, u32[]{:S(2)}) copy-start(f32[1,256,768]{2,1,0:T(8,128)} %copy-done.12) | copy-start | bytes 2359300
  260.9 40.3 %copy-start.72 = (f32[768]{0:T(1024)S(1)}, f32[768]{0:T(1024)}, u32[]{:S(2)}) copy-start(f32[768]{0:T(1024)} %get-tuple-element.141) | copy-start | bytes 9220
  260.9 42.0 %copy-start.63 = (f32[512,96]{0,1:T(8,128)S(1)}, f32[512,96]{0,1:T(8,128)}, u32[]{:S(2)}) copy-start(f32[512,96]{0,1:T(8,128)} %param.40) | copy-start | bytes 589828
  260.9 87.0 %all-gather.17.cloned.1.call-start = ((), (), s32[]{:S(2)}) async-start(), calls=%async_computation.18 | async-start | bytes 1769472 | tf_op jit(solution)/shard_map/all_gather | solution.py:207
  261.7 107.4 %all-gather.15.cloned.1.call-start = ((), (), s32[]{:S(2)}) async-start(), calls=%async_computation.17 | async-start | bytes 1966080 | tf_op jit(solution)/shard_map/all_gather | solution.py:36
  302.2 88.2 %all-gather.19.cloned.1.call-start = ((), (), s32[]{:S(2)}) async-start(), calls=%async_computation.20 | async-start | bytes 1966080 | tf_op jit(solution)/shard_map/all_gather | solution.py:40
  302.9 135.0 %reduce-scatter.25.cloned.1.call-start = ((), (), s32[]{:S(2)}) async-start(), calls=%async_computation.21 | async-start | bytes 3932160 | tf_op jit(solution)/shard_map/reduce_scatter | solution.py:48
  336.0 54.3 %copy-start.35 = (bf16[512,768]{0,1:T(8,128)(2,1)}, bf16[512,768]{0,1:T(8,128)(2,1)S(1)}, u32[]{:S(2)}) copy-start(bf16[512,768]{0,1:T(8,128)(2,1)S(1)} %all_gather.43) | copy-start | bytes 2359300
  399.8 38.1 %copy-start.16 = (f32[1,256,768]{2,1,0:T(8,128)S(1)}, f32[1,256,768]{2,1,0:T(8,128)}, u32[]{:S(2)}) copy-start(f32[1,256,768]{2,1,0:T(8,128)} %copy-done.15) | copy-start | bytes 2359300
  399.8 40.1 %copy-start.32 = (bf16[1,256,768]{2,1,0:T(8,128)(2,1)S(1)}, bf16[1,256,768]{2,1,0:T(8,128)(2,1)}, u32[]{:S(2)}) copy-start(bf16[1,256,768]{2,1,0:T(8,128)(2,1)} %param.24) | copy-start | bytes 1179652
  399.8 62.1 %copy-start.53 = (bf16[1,192,768]{2,1,0:T(8,128)(2,1)S(1)}, bf16[1,192,768]{2,1,0:T(8,128)(2,1)}, u32[]{:S(2)}) copy-start(bf16[1,192,768]{2,1,0:T(8,128)(2,1)} %copy-done.52) | copy-start | bytes 884740
  399.8 62.0 %all-gather.21.cloned.1.call-start = ((), (), s32[]{:S(2)}) async-start(), calls=%async_computation.22 | async-start | bytes 1966080 | tf_op jit(solution)/shard_map/all_gather | solution.py:40
  442.0 140.4 %reduce-scatter.27.cloned.1.call-start = ((), (), s32[]{:S(2)}) async-start(), calls=%async_computation.23 | async-start | bytes 1966080 | tf_op jit(solution)/shard_map/reduce_scatter | solution.py:290
  463.9 19.6 %copy-start.41 = (bf16[1024,192]{0,1:T(8,128)(2,1)}, bf16[1024,192]{0,1:T(8,128)(2,1)S(1)}, u32[]{:S(2)}) copy-start(bf16[1024,192]{0,1:T(8,128)(2,1)S(1)} %fusion.107) | copy-start | bytes 1179652
  554.1 68.7 %reduce-scatter.23.cloned.1.call-start = ((), (), s32[]{:S(2)}) async-start(), calls=%async_computation.19 | async-start | bytes 3932160 | tf_op jit(solution)/shard_map/reduce_scatter | solution.py:44
  554.2 28.3 %copy-start.14 = (f32[1,256,768]{2,1,0:T(8,128)S(1)}, f32[1,256,768]{2,1,0:T(8,128)}, u32[]{:S(2)}) copy-start(f32[1,256,768]{2,1,0:T(8,128)} %copy-done.12) | copy-start | bytes 2359300
  554.2 28.3 %copy-start.80 = (f32[768]{0:T(1024)S(1)}, f32[768]{0:T(1024)}, u32[]{:S(2)}) copy-start(f32[768]{0:T(1024)} %copy-done.79) | copy-start | bytes 9220
  554.2 28.3 %copy-start.90 = (f32[256]{0:T(256)S(1)}, f32[256]{0:T(256)}, u32[]{:S(2)}) copy-start(f32[256]{0:T(256)} %copy-done.89) | copy-start | bytes 3076
  558.4 25.3 %copy-start.93 = (f32[256]{0:T(256)S(1)}, f32[256]{0:T(256)}, u32[]{:S(2)}) copy-start(f32[256]{0:T(256)} %copy-done.92) | copy-start | bytes 3076
  558.4 156.8 %all-gather.23.cloned.1.call-start = ((), (), s32[]{:S(2)}) async-start(), calls=%async_computation.24 | async-start | bytes 1966080 | tf_op jit(solution)/shard_map/all_gather | solution.py:40
  626.2 147.6 %reduce-scatter.35.cloned.1.call-start = ((), (), s32[]{:S(2)}) async-start(), calls=%async_computation.28 | async-start | bytes 1769472 | tf_op jit(solution)/shard_map/reduce_scatter | solution.py:336
  630.3 160.9 %reduce-scatter.33.cloned.1.call-start = ((), (), s32[]{:S(2)}) async-start(), calls=%async_computation.27 | async-start | bytes 3538944 | tf_op jit(solution)/shard_map/reduce_scatter | solution.py:335
  639.8 11.1 %copy-start.57 = (bf16[1024,512]{1,0:T(8,128)(2,1)S(1)}, bf16[1024,512]{1,0:T(8,128)(2,1)}, u32[]{:S(2)}) copy-start(bf16[1024,512]{1,0:T(8,128)(2,1)} %copy-done.56) | copy-start | bytes 3145732
  656.5 201.0 %reduce-scatter.39.cloned.1.call-start = ((), (), s32[]{:S(2)}) async-start(), calls=%async_computation.30 | async-start | bytes 1327104
  667.6 24.7 %slice-start.13 = ((s8[6291456]{0:T(1024)(128)(4,1)}), s8[4194304]{0:T(1024)(128)(4,1)S(1)}, s32[]{:S(2)}) async-start(s8[6291456]{0:T(1024)(128)(4,1)} %bitcast.365), calls=%async_computation.45 | async-start | bytes 8388608
  678.6 13.8 %slice-start.14 = ((s8[6291456]{0:T(1024)(128)(4,1)}), s8[2097152]{0:T(1024)(128)(4,1)S(1)}, s32[]{:S(2)}) async-start(s8[6291456]{0:T(1024)(128)(4,1)} %bitcast.365), calls=%async_computation.46 | async-start | bytes 4194304
  692.4 10.1 slice-start.8
  692.4 10.1 slice-start.9
  711.8 212.1 %reduce-scatter.41.cloned.1.call-start = ((), (), s32[]{:S(2)}) async-start(), calls=%async_computation.31 | async-start | bytes 1327104
  722.6 9.2 slice-start.4
  731.8 10.6 copy-start.43
  731.8 13.4 %slice-start.2 = ((s8[6291456]{0:T(1024)(128)(4,1)}), s8[2097152]{0:T(1024)(128)(4,1)S(1)}, s32[]{:S(2)}) async-start(s8[6291456]{0:T(1024)(128)(4,1)} %bitcast.353), calls=%async_computation.34 | async-start | bytes 4194304
  735.5 259.8 %reduce-scatter.37.cloned.1.call-start = ((), (), s32[]{:S(2)}) async-start(), calls=%async_computation.29 | async-start | bytes 2654208
  735.5 8.5 slice-start.6
  735.6 8.5 slice-start.7
  735.6 9.7 slice-start.3
  757.6 277.2 %reduce-scatter.29.cloned.1.call-start = ((), (), s32[]{:S(2)}) async-start(), calls=%async_computation.25 | async-start | bytes 3932160 | tf_op jit(solution)/shard_map/reduce_scatter | solution.py:48
  763.0 336.8 %reduce-scatter.31.cloned.1.call-start = ((), (), s32[]{:S(2)}) async-start(), calls=%async_computation.26 | async-start | bytes 7864320 | tf_op jit(solution)/shard_map/reduce_scatter | solution.py:293
  773.3 261.5 %copy-start.22 = (bf16[1,256,768]{2,1,0:T(8,128)(2,1)S(1)}, bf16[1,256,768]{2,1,0:T(8,128)(2,1)}, u32[]{:S(2)}) copy-start(bf16[1,256,768]{2,1,0:T(8,128)(2,1)} %param.23) | copy-start | bytes 1179652
  773.3 261.5 %copy-start.78 = (f32[768]{0:T(1024)S(1)}, f32[768]{0:T(1024)}, u32[]{:S(2)}) copy-start(f32[768]{0:T(1024)} %copy-done.77) | copy-start | bytes 9220
  773.3 261.5 %copy-start.87 = (f32[256]{0:T(256)S(1)}, f32[256]{0:T(256)}, u32[]{:S(2)}) copy-start(f32[256]{0:T(256)} %copy-done.86) | copy-start | bytes 3076
  773.6 263.2 %copy-start.69 = (f32[4,96,192]{2,1,0:T(8,128)S(1)}, f32[4,96,192]{2,1,0:T(8,128)}, u32[]{:S(2)}) copy-start(f32[4,96,192]{2,1,0:T(8,128)} %param.30) | copy-start | bytes 884740
  860.0 176.8 %copy-start.91 = (f32[1,768]{1,0:T(1,128)S(1)}, f32[1,768]{1,0:T(1,128)}, u32[]{:S(2)}) copy-start(f32[1,768]{1,0:T(1,128)} %stack.69) | copy-start | bytes 9220
  1080.5 12.2 %copy-start.62 = (f32[2,192,96]{2,1,0:T(8,128)S(1)}, f32[2,192,96]{2,1,0:T(8,128)}, u32[]{:S(2)}) copy-start(f32[2,192,96]{2,1,0:T(8,128)} %param.34) | copy-start | bytes 442372
  1083.2 13.7 %copy-start.36 = (f32[1,256,768]{2,1,0:T(8,128)S(1)}, f32[1,256,768]{2,1,0:T(8,128)}, u32[]{:S(2)}) copy-start(f32[1,256,768]{2,1,0:T(8,128)} %get-tuple-element.170) | copy-start | bytes 2359300
  1083.2 13.7 %copy-start.37 = (f32[1,256,768]{2,1,0:T(8,128)S(1)}, f32[1,256,768]{2,1,0:T(8,128)}, u32[]{:S(2)}) copy-start(f32[1,256,768]{2,1,0:T(8,128)} %reduce-scatter.29.cloned.1.call-done) | copy-start | bytes 2359300
  1089.7 8.8 copy-start.47
  1089.7 8.8 copy-start.48
  1090.6 7.9 copy-start.67
  (69 other events, 230.8 us)
Sparse Core Ops, SparseCore 0:
  10.8 50.6 all-gather.10
  63.6 19.2 all-gather.8
  102.3 37.9 reduce-scatter.18
  143.5 19.6 all-gather.12
  261.1 37.9 reduce-scatter.20
  301.7 46.2 all-gather.16
  350.1 18.9 all-gather.14
  370.7 19.6 all-gather.18
  399.9 37.9 reduce-scatter.24
  442.2 19.6 all-gather.20
  554.2 28.1 reduce-scatter.26
  584.8 37.9 reduce-scatter.22
  626.3 19.6 all-gather.22
  649.6 64.9 reduce-scatter.34
  718.0 73.0 reduce-scatter.32
  794.4 63.1 reduce-scatter.38
  860.8 63.0 reduce-scatter.40
  927.2 67.9 reduce-scatter.36
  997.8 36.9 reduce-scatter.28
  1038.0 59.0 reduce-scatter.30
where the time goes:
time: 1120 us; the launch traced here: 1110 us
  waiting for transfers between devices  522 us (47%)
  matrix products  260 us (23%)
  blocking collectives  140 us (12%)
  other arithmetic  112 us (10%)
  local copies, waits for them, and re-layouts  50.7 us (5%)
  between operations  22.1 us (2%)
    unnamed x23, waiting for transfers between devices  199 us
    reduce_scatter x3, waiting for transfers between devices, sum_branch(): lax.psum_scatter(partial_out, 'tensor', scatter_dimension=1, tiled=True)  114 us
    reduce_scatter x2, waiting for transfers between devices, sum_inputs(): lax.psum_scatter(partial_grad, 'tensor', scatter_dimension=1, tiled=True)  72.2 us
    unnamed x255, local copies, waits for them, and re-layouts  47.5 us
    dot_general x4, matrix products, attend_backward(): jnp.einsum('rqhd,rkhd->rhqk', grad_block, values_all, preferred_element_t...  43.1 us
    all_gather x3, waiting for transfers between devices, spread_rows(): return lax.all_gather(normed, 'tensor', axis=1, tiled=True)  42.6 us
    convert_element_type x4, other arithmetic, attend_backward(): score_grad = (probabilities * (prob_grad - inner_sum)).astype(jnp.bfloat16)  41.2 us
    psum x1, blocking collectives, local(): lax.psum((gain_grads, local_squares), ('dp', 'tensor'))  39.8 us
  transfers between devices with their start and end apart: 20, of which 16 were waited for; matrix products, arithmetic and copies ran while one was open for 19% of the time, Pallas kernels for 0%

commit v1 on v0

v1 whole, which is shorter than its diff:
```python
import functools

import jax
import jax.numpy as jnp
from jax import lax
from jax.experimental import pallas as pl
from jax.experimental.pallas import tpu as pltpu
from jax.sharding import PartitionSpec as P

HEAD = 64
SEGS = 4
STEP = 10
NORM_EPS = 1e-06
ADAM_EPS = 1e-08
BETA_ONE = 0.9
BETA_TWO = 0.999
DECAY = 0.1
RATE_INNER = 0.05
RATE_OUTER = 0.4
RATE_GAIN = 0.5
CLIP = 1.0
MASKED = -1e30
SCALE = HEAD ** (-0.5)

MESH = pl.DeviceIdType.MESH
BF = jnp.bfloat16
F32 = jnp.float32
VLIMIT = 58 * 2**20
VM = pl.BlockSpec(memory_space=pltpu.VMEM)
ANY = pl.BlockSpec(memory_space=pl.ANY)
SM = pl.BlockSpec(memory_space=pltpu.SMEM)
DMA = pltpu.SemaphoreType.DMA


def sds(shape, dtype):
    return jax.ShapeDtypeStruct(shape, dtype)


def nn(a, b):
    return lax.dot_general(a, b, (((1,), (0,)), ((), ())), preferred_element_type=F32)


def nt(a, b):
    return lax.dot_general(a, b, (((1,), (1,)), ((), ())), preferred_element_type=F32)


def rows(i, size):
    return pl.ds(pl.multiple_of(i * size, size), size)


def flat(ref):
    return ref[...].reshape(ref.shape[0] * ref.shape[1], ref.shape[2])


def norm(v, g):
    return v * lax.rsqrt(jnp.mean(v * v, axis=-1, keepdims=True) + NORM_EPS) * g


def norm_back(v, g, dy):
    r = lax.rsqrt(jnp.mean(v * v, axis=-1, keepdims=True) + NORM_EPS)
    n = v * r
    dn = dy * g
    dv = r * (dn - n * jnp.mean(dn * n, axis=-1, keepdims=True))
    return dv, jnp.sum(dy * n, axis=0, keepdims=True)


class Place:
    def __init__(self, n):
        self.n = n
        self.d = lax.axis_index("dp")
        self.t = lax.axis_index("tensor")
        self.tc = self.t + 1 - 2 * lax.rem(self.t, 2)
        self.ty = lax.rem(self.t + 2, 4)
        self.tcy = lax.rem(self.tc + 2, 4)
        self.core = (self.d, self.tc)
        self.y = (self.d, self.ty)
        self.dx = self.d + 1 - 2 * lax.rem(self.d, 2)
        self.x = (self.dx, self.t)

    def z(self, k):
        return (lax.rem(self.d + 2 * k, self.n), self.t)

    def from_z(self, k):
        return lax.rem(self.d - 2 * k + 2 * self.n, self.n)

    def x_from_z(self, k):
        return lax.rem(self.dx - 2 * k + 2 * self.n, self.n)


def greet(devices):
    bar = pltpu.get_barrier_semaphore()
    for dev in devices:
        pl.semaphore_signal(bar, inc=1, device_id=dev, device_id_type=MESH)
    pl.semaphore_wait(bar, len(devices))


def rcopy(src, dst, ss, rs, dev):
    return pltpu.make_async_remote_copy(
        src_ref=src, dst_ref=dst, send_sem=ss, recv_sem=rs, device_id=dev, device_id_type=MESH
    )


class TensorSum:
    def __init__(self, place, refs):
        self.p = place
        self.s0, self.s1, self.r0, self.r1, self.own, self.ys, self.yr, self.ss, self.rs = refs

    @staticmethod
    def scratch(tile, width, hop=F32):
        return [pltpu.VMEM((tile, width), hop)] * 4 + [
            pltpu.VMEM((tile, width), F32),
            pltpu.VMEM((tile, width), BF),
            pltpu.VMEM((tile, width), BF),
            DMA((3,)),
            DMA((3,)),
        ]

    def begin(self, tile_fn):
        p = self.p
        self.c0 = rcopy(self.s0, self.r0, self.ss.at[0], self.rs.at[0], p.core)
        self.c1 = rcopy(self.s1, self.r1, self.ss.at[1], self.rs.at[1], p.core)
        self.cy = rcopy(self.ys, self.yr, self.ss.at[2], self.rs.at[2], p.y)
        self.s0[...] = tile_fn(p.tcy).astype(self.s0.dtype)
        self.c0.start()
        part = tile_fn(p.ty)
        self.c0.wait_recv()
        self.ys[...] = (part + self.r0[...].astype(F32)).astype(BF)
        self.cy.start()
        self.s1[...] = tile_fn(p.tc).astype(self.s1.dtype)
        self.c1.start()
        self.own[...] = tile_fn(p.t)

    def end(self):
        self.c1.wait_recv()
        self.cy.wait_recv()
        total = self.own[...] + self.r1[...].astype(F32) + self.yr[...].astype(F32)
        self.c0.wait_send()
        self.c1.wait_send()
        self.cy.wait_send()
        return total


class TensorGather:
    def __init__(self, place, full, sems, tile):
        self.p = place
        self.full = full
        self.tile = tile
        ss, rs = sems
        p = place
        mine = full.at[rows(p.t, tile)]
        far = full.at[rows(p.ty, tile)]
        self.cc = rcopy(mine, mine, ss.at[0], rs.at[0], p.core)
        self.cy = rcopy(mine, mine, ss.at[1], rs.at[1], p.y)
        self.cf = rcopy(far, far, ss.at[2], rs.at[2], p.core)
        near = full.at[rows(p.tc, tile)]
        cross = full.at[rows(p.tcy, tile)]
        self.wc = rcopy(near, near, ss.at[0], rs.at[0], p.core)
        self.wy = rcopy(far, far, ss.at[1], rs.at[1], p.y)
        self.wf = rcopy(cross, cross, ss.at[2], rs.at[2], p.core)

    @staticmethod
    def scratch():
        return [DMA((3,)), DMA((3,))]

    def begin(self, own):
        self.full[rows(self.p.t, self.tile), :] = own
        self.cy.start()
        self.cc.start()

    def forward(self):
        self.wy.wait_recv()
        self.cf.start()

    def end(self):
        self.wc.wait_recv()
        self.wf.wait_recv()
        self.cy.wait_send()
        self.cc.wait_send()
        self.cf.wait_send()


class RowGather:
    def __init__(self, place, full, sems):
        self.p = place
        self.full = full
        self.zs, self.zr, self.xs, self.xr = sems
        self.steps = place.n // 2

    @staticmethod
    def scratch(n):
        return [DMA((n // 2,))] * 4

    def zcopy(self, k, slot):
        return rcopy(self.full.at[slot], self.full.at[slot], self.zs.at[k], self.zr.at[k], self.p.z(k))

    def xcopy(self, k, slot):
        return rcopy(self.full.at[slot], self.full.at[slot], self.xs.at[k], self.xr.at[k], self.p.x)

    def begin(self):
        for k in range(1, self.steps):
            self.zcopy(k, self.p.d).start()
        self.xcopy(0, self.p.d).start()

    def sent(self):
        for k in range(1, self.steps):
            self.zcopy(k, self.p.d).wait_send()

    def forward(self):
        for k in range(1, self.steps):
            slot = self.p.from_z(k)
            self.zcopy(k, slot).wait_recv()
            self.xcopy(k, slot).start()

    def end(self):
        for k in range(self.steps):
            self.xcopy(k, self.p.x_from_z(k)).wait_recv()
            self.xcopy(k, self.p.from_z(k)).wait_send()


def head_rows(qt, head):
    ids = lax.broadcasted_iota(jnp.int32, qt.shape, 0)
    return jnp.where((ids >= head * HEAD) & (ids < (head + 1) * HEAD), qt, 0.0).astype(BF)


def head_block(x, heads):
    ids = lax.broadcasted_iota(jnp.int32, x.shape, 1)
    return jnp.concatenate(
        [jnp.where((ids >= h * HEAD) & (ids < (h + 1) * HEAD), x, 0.0).astype(BF) for h in range(heads)], axis=0
    )


def segment_starts(seg):
    start = jnp.zeros(seg.shape, jnp.int32)
    for s in range(SEGS - 1):
        count = jnp.sum(jnp.where(seg == s, 1, 0), axis=1, keepdims=True)
        start = start + jnp.where(seg > s, count, 0)
    return start


def causal_mask(keys, tile, tau, start):
    key_place = lax.broadcasted_iota(jnp.int32, (keys, tile), 0)
    query_place = lax.broadcasted_iota(jnp.int32, (keys, tile), 1) + tau * tile
    return (key_place <= query_place) & (key_place >= start)


def first_kernel(n, gather, heads, x0_ref, cot_ref, gain_ref, seg_ref, sa_ref, sb_ref, sc_ref, m_hbm,
                 qkv_ref, qkvt_ref, a_ref, at_ref, lse_ref, x1_ref, qc_ref, qct_ref,
                 ga_out, gb_out, gc_out, h0_out, h1_out, e3_out, kv_out, kvt_out,
                 ga, gb, gc, h0, h1, e3, kv, kvt, m_ref, lsem, osem, *rest):
    rest = list(rest)

    def take(count):
        got = rest[:count]
        del rest[:count]
        return got

    p = Place(n)
    tile = x0_ref.shape[0]
    width = heads * HEAD
    tiles = h0.shape[0] // tile
    load_m = pltpu.make_async_copy(m_hbm, m_ref, lsem.at[0])
    load_m.start()
    sum_refs = take(9)
    gathers = [TensorGather(p, full, take(2), tile) for full in (h0, e3, h1)]
    if gather:
        parts = [RowGather(p, full, take(4)) for full in (ga, gb, gc)]
        for full, shard in ((ga, sa_ref), (gb, sb_ref), (gc, sc_ref)):
            full[p.d] = shard[...]
        greet([p.core, p.y, p.x] + [p.z(k) for k in range(1, n // 2)])
        parts[0].begin()
    else:
        copies = [pltpu.make_async_copy(s, f, lsem.at[1 + i]) for i, (s, f) in
                  enumerate(((sa_ref, ga), (sb_ref, gb), (sc_ref, gc)))]
        for c in copies:
            c.start()
        greet([p.core, p.y])

    x0 = x0_ref[...].astype(F32)
    gathers[0].begin(norm(x0, gain_ref[0:1, :]).astype(BF))
    start = segment_starts(seg_ref[...])
    if gather:
        parts[0].forward()
        parts[1].begin()
    gathers[0].forward()
    gathers[1].begin(cot_ref[...])
    gathers[0].end()
    if gather:
        parts[0].end()
    else:
        for c in copies:
            c.wait()

    wa = flat(ga)
    for i in range(tiles):
        at = slice(i * tile, (i + 1) * tile)
        x = nn(h0[at, :], wa[:, : 3 * width])
        qkv_ref[at, :] = x.astype(BF)
        qkvt_ref[:, at] = x.T.astype(BF)
    outs = []

    def put(src, dst):
        c = pltpu.make_async_copy(src, dst, osem.at[len(outs)])
        c.start()
        outs.append(c)

    put(ga, ga_out)
    put(h0, h0_out)
    if gather:
        parts[1].forward()
        parts[2].begin()
    gathers[1].forward()

    for i in range(tiles):
        at = slice(i * tile, (i + 1) * tile)
        keys = (i + 1) * tile
        kk = qkv_ref[0:keys, width : 2 * width]
        qt = qkvt_ref[0:width, at].astype(F32) * SCALE
        allowed = causal_mask(keys, tile, i, start[:, at])
        for h in range(heads):
            s = jnp.where(allowed, nn(kk, head_rows(qt, h)), MASKED)
            peak = jnp.max(s, axis=0, keepdims=True)
            e = jnp.exp(s - peak)
            total = jnp.sum(e, axis=0, keepdims=True)
            w = (e * (1.0 / total)).astype(BF)
            vt = qkvt_ref[2 * width + h * HEAD : 2 * width + (h + 1) * HEAD, 0:keys]
            at_ref[h * HEAD : (h + 1) * HEAD, at] = nn(vt, w)
            lse_ref[h : h + 1, at] = peak + jnp.log(total)
        a_ref[at, :] = at_ref[:, at].T.astype(BF)

    if gather:
        parts[1].end()
    gathers[1].end()
    put(gb, gb_out)
    put(e3, e3_out)
    wb = flat(gb)
    wo = wb[:, 2 * width : 3 * width]
    total = TensorSum(p, sum_refs)
    total.begin(lambda j: nt(a_ref[rows(j, tile), :], wo))
    load_m.wait()
    mtiles = m_ref.shape[0] // 256

    def project_memory(i, carry):
        x = nn(m_ref[rows(i, 256), :], flat(gb)[:, : 2 * width])
        kv[rows(i, 256), :] = x.astype(BF)
        kvt[:, rows(i, 256)] = x.T.astype(BF)
        return carry

    lax.fori_loop(0, mtiles // 2, project_memory, 0)
    if gather:
        parts[2].forward()
    x1 = x0 + total.end()
    x1_ref[...] = x1
    gathers[2].begin(norm(x1, gain_ref[1:2, :]).astype(BF))
    lax.fori_loop(mtiles // 2, mtiles, project_memory, 0)
    put(kv, kv_out)
    put(kvt, kvt_out)
    gathers[2].forward()
    gathers[2].end()
    put(h1, h1_out)
    wq = flat(ga)[:, 3 * width : 4 * width]
    for i in range(tiles):
        at = slice(i * tile, (i + 1) * tile)
        x = nn(h1[at, :], wq)
        qc_ref[at, :] = x.astype(BF)
        qct_ref[:, at] = x.T.astype(BF)
    if gather:
        for part in parts:
            part.sent()
        parts[2].end()
    put(gc, gc_out)
    for c in outs:
        c.wait()


def call_first(n, gather, x0, cot, gain, seg, sa, sb, sc, mem):
    tile, width_d = x0.shape
    length = seg.shape[1]
    states = mem.shape[0]
    cols = sa.shape[-1]
    width = cols // 4
    heads = width // HEAD
    chunk = (8, width_d // 8)
    shapes = [chunk + (s.shape[-1],) for s in (sa, sb, sc)]
    out_shape = [
        sds((length, 3 * width), BF),
        sds((3 * width, length), BF),
        sds((length, width), BF),
        sds((width, length), F32),
        sds((8, length), F32),
        sds((tile, width_d), F32),
        sds((length, width), BF),
        sds((width, length), BF),
        sds(shapes[0], BF),
        sds(shapes[1], BF),
        sds(shapes[2], BF),
        sds((length, width_d), BF),
        sds((length, width_d), BF),
        sds((length, width_d), BF),
        sds((states, 2 * width), BF),
        sds((2 * width, states), BF),
    ]
    scratch = [pltpu.VMEM(s, BF) for s in shapes]
    scratch += [pltpu.VMEM((length, width_d), BF)] * 3
    scratch += [
        pltpu.VMEM((states, 2 * width), BF),
        pltpu.VMEM((2 * width, states), BF),
        pltpu.VMEM((states, width_d), BF),
        DMA((4,)),
        DMA((8,)),
    ]
    scratch += TensorSum.scratch(tile, width_d)
    scratch += TensorGather.scratch() * 3
    if gather:
        scratch += RowGather.scratch(n) * 3
    shard = VM if gather else ANY
    return pl.pallas_call(
        functools.partial(first_kernel, n, gather, heads),
        out_shape=out_shape,
        in_specs=[VM, VM, VM, VM, shard, shard, shard, ANY],
        out_specs=[VM] * 8 + [ANY] * 8,
        scratch_shapes=scratch,
        compiler_params=pltpu.CompilerParams(collective_id=1, has_side_effects=True, vmem_limit_bytes=VLIMIT),
        name="self_forward",
    )(x0, cot, gain, seg, sa, sb, sc, mem)


def cross_forward_kernel(heads, plots, flags_ref, tp_ref, qct_ref, kv_ref, kvt_ref, ct_ref, c_ref, lse_ref, vte):
    width = heads * HEAD
    states = kv_ref.shape[0]
    patches = states // plots
    length = qct_ref.shape[1]
    tile = 256
    chunk = 512
    ext = HEAD + 16
    for h in range(heads):
        vte[h * ext : h * ext + HEAD, :] = kvt_ref[width + h * HEAD : width + (h + 1) * HEAD, :]
        vte[h * ext + HEAD : (h + 1) * ext, :] = jnp.ones((16, states), BF)
    ct_ref[...] = jnp.zeros(ct_ref.shape, F32)
    lse_ref[...] = jnp.zeros(lse_ref.shape, F32)

    def one_tile(i, carry):
        at = rows(i, tile)
        qt = qct_ref[:, at].astype(F32) * SCALE
        qh = [head_rows(qt, h) for h in range(heads)]
        tags = tp_ref[:, at]
        for plot in range(plots):

            @pl.when(flags_ref[i * plots + plot] != 0)
            def _():
                def one_chunk(j, state):
                    place = rows(plot * (patches // chunk) + j, chunk)
                    kk = kv_ref[place, 0:width]
                    new = []
                    for h in range(heads):
                        peak, acc = state[2 * h], state[2 * h + 1]
                        s = nn(kk, qh[h])
                        peak_new = jnp.maximum(peak, jnp.max(s, axis=0, keepdims=True))
                        e = jnp.exp(s - peak_new).astype(BF)
                        acc = acc * jnp.exp(peak - peak_new) + nn(vte[h * ext : (h + 1) * ext, place], e)
                        new += [peak_new, acc]
                    return tuple(new)

                init = (jnp.full((1, tile), MASKED, F32), jnp.zeros((ext, tile), F32)) * heads
                state = lax.fori_loop(0, patches // chunk, one_chunk, init)
                sel = tags == plot
                for h in range(heads):
                    peak, acc = state[2 * h], state[2 * h + 1]
                    total = acc[HEAD : HEAD + 1, :]
                    hs = slice(h * HEAD, (h + 1) * HEAD)
                    ct_ref[hs, at] = jnp.where(sel, acc[0:HEAD, :] * (1.0 / total), ct_ref[hs, at])
                    lse_ref[h : h + 1, at] = jnp.where(sel, peak + jnp.log(total), lse_ref[h : h + 1, at])

        c_ref[at, :] = ct_ref[:, at].T.astype(BF)
        return carry

    lax.fori_loop(0, length // tile, one_tile, 0)


def call_cross_forward(plots, flags, tp, qct, kv, kvt):
    width, length = qct.shape
    heads = width // HEAD
    return pl.pallas_call(
        functools.partial(cross_forward_kernel, heads, plots),
        out_shape=[sds((width, length), F32), sds((length, width), BF), sds((8, length), F32)],
        in_specs=[SM] + [VM] * 4,
        out_specs=[VM] * 3,
        scratch_shapes=[pltpu.VMEM((heads * (HEAD + 16), kv.shape[0]), BF)],
        compiler_params=pltpu.CompilerParams(vmem_limit_bytes=VLIMIT),
        name="cross_forward",
    )(flags, tp, qct, kv, kvt)


def ffn_kernel(n, heads, c_ref, x1_ref, gain_ref, gb_ref, gc_ref, e3_ref,
               x2_ref, out_ref, g2_ref, e2_ref, dgain_ref, du_ref,
               h2, f, dg, h2t, e3t, *rest):
    rest = list(rest)

    def take(count):
        got = rest[:count]
        del rest[:count]
        return got

    p = Place(n)
    tile, width_d = x1_ref.shape
    width = heads * HEAD
    hidden = f.shape[1]
    sums = [TensorSum(p, take(9)) for _ in range(3)]
    gathers = [TensorGather(p, full, take(2), tile) for full in (h2, e2_ref)]
    greet([p.core, p.y])
    wo = flat(gb_ref)[:, 3 * width : 4 * width]
    sums[0].begin(lambda j: nt(c_ref[rows(j, tile), :], wo))
    e3t[...] = e3_ref[...].T
    x2 = x1_ref[...] + sums[0].end()
    x2_ref[...] = x2
    gathers[0].begin(norm(x2, gain_ref[2:3, :]).astype(BF))

    def hidden_tile(j):
        at = rows(j, tile)
        gate = nn(h2[at, :], flat(gc_ref)[:, 0:hidden])
        up = nn(h2[at, :], flat(gc_ref)[:, hidden : 2 * hidden])
        df = nn(e3_ref[at, :], flat(gc_ref)[:, 2 * hidden : 3 * hidden])
        sq = gate * gate
        th = jnp.tanh(0.7978845608 * gate * (1.0 + 0.044715 * sq))
        half = 0.5 * (1.0 + th)
        act = gate * half
        slope = half + 0.5 * gate * (1.0 - th * th) * (0.7978845608 * (1.0 + 3.0 * 0.044715 * sq))
        f[at, :] = (act * up).astype(BF)
        dg[at, 0:hidden] = (df * up * slope).astype(BF)
        dg[at, hidden : 2 * hidden] = (df * act).astype(BF)

    hidden_tile(p.t)
    gathers[0].wc.wait_recv()
    hidden_tile(p.tc)
    gathers[0].forward()
    hidden_tile(p.ty)
    gathers[0].wf.wait_recv()
    hidden_tile(p.tcy)
    gathers[0].cy.wait_send()
    gathers[0].cc.wait_send()
    gathers[0].cf.wait_send()
    sums[1].begin(lambda j: nt(dg[rows(j, tile), :], flat(gc_ref)[:, 0 : 2 * hidden]))
    h2t[...] = h2[...].T
    for i in range(2 * hidden // 256):
        cs = slice(i * 256, (i + 1) * 256)
        du_ref[:, cs] = nn(h2t[...], dg[:, cs]).astype(BF)
    dh2 = sums[1].end()
    dv, dgain = norm_back(x2, gain_ref[2:3, :], dh2)
    dgain_ref[...] = dgain
    g2 = e3_ref[rows(p.t, tile), :].astype(F32) + dv
    g2_ref[...] = g2
    gathers[1].begin(g2.astype(BF))
    sums[2].begin(lambda j: nt(f[rows(j, tile), :], flat(gc_ref)[:, 2 * hidden : 3 * hidden]))
    gathers[1].forward()
    for i in range(hidden // 256):
        cs = slice(i * 256, (i + 1) * 256)
        du_ref[:, 2 * hidden + i * 256 : 2 * hidden + (i + 1) * 256] = nn(e3t[...], f[:, cs]).astype(BF)
    gathers[1].end()
    out_ref[...] = (x2 + sums[2].end()).astype(BF)


def call_ffn(n, c, x1, gain, gb, gc, e3):
    tile, width_d = x1.shape
    length, width = c.shape
    hidden = gc.shape[2] // 3
    scratch = [
        pltpu.VMEM((length, width_d), BF),
        pltpu.VMEM((length, hidden), BF),
        pltpu.VMEM((length, 2 * hidden), BF),
        pltpu.VMEM((width_d, length), BF),
        pltpu.VMEM((width_d, length), BF),
    ]
    scratch += TensorSum.scratch(tile, width_d) * 3 + TensorGather.scratch() * 2
    return pl.pallas_call(
        functools.partial(ffn_kernel, n, width // HEAD),
        out_shape=[
            sds((tile, width_d), F32),
            sds((tile, width_d), BF),
            sds((tile, width_d), F32),
            sds((length, width_d), BF),
            sds((1, width_d), F32),
            sds((width_d, 3 * hidden), BF),
        ],
        in_specs=[VM] * 6,
        out_specs=[VM] * 6,
        scratch_shapes=scratch,
        compiler_params=pltpu.CompilerParams(collective_id=2, has_side_effects=True, vmem_limit_bytes=VLIMIT),
        name="ffn",
    )(c, x1, gain, gb, gc, e3)


def cross_backward_kernel(heads, plots, flags_ref, tp_ref, e2_ref, gb_ref, qc_ref, qct_ref, kv_ref, kvt_ref,
                          ct_ref, lse_ref, dqc_ref, dk_ref, dv_ref, dka, dva, dqt, vrow):
    width = heads * HEAD
    states = kv_ref.shape[0]
    patches = states // plots
    length = qct_ref.shape[1]
    tile = 256
    chunk = 512
    dka[...] = jnp.zeros(dka.shape, F32)
    dva[...] = jnp.zeros(dva.shape, F32)
    vrow[...] = kv_ref[:, width : 2 * width]

    def one_tile(i, carry):
        at = rows(i, tile)
        dc = nn(e2_ref[at, :], flat(gb_ref)[:, 3 * width : 4 * width])
        dcr = dc.astype(BF)
        dct = dc.T.astype(BF).astype(F32)
        qt = qct_ref[:, at].astype(F32) * SCALE
        qh = [head_rows(qt, h) for h in range(heads)]
        dh = [head_rows(dct, h) for h in range(heads)]
        inner = [
            jnp.sum(dct[h * HEAD : (h + 1) * HEAD, :] * ct_ref[h * HEAD : (h + 1) * HEAD, at], axis=0, keepdims=True)
            for h in range(heads)
        ]
        qb = head_block(qc_ref[at, :].astype(F32) * SCALE, heads)
        db = head_block(dcr.astype(F32), heads)
        tags = tp_ref[:, at]
        dqt[...] = jnp.zeros(dqt.shape, F32)
        for plot in range(plots):

            @pl.when(flags_ref[i * plots + plot] != 0)
            def _():
                lse = [jnp.where(tags == plot, lse_ref[h : h + 1, at], -MASKED) for h in range(heads)]

                def one_chunk(j, carry):
                    place = rows(plot * (patches // chunk) + j, chunk)
                    kk = kv_ref[place, 0:width]
                    vv = vrow[place, :]
                    ps, ds = [], []
                    for h in range(heads):
                        prob = jnp.exp(nn(kk, qh[h]) - lse[h])
                        grad = (prob * (nn(vv, dh[h]) - inner[h])).astype(BF)
                        ps.append(prob.astype(BF))
                        ds.append(grad)
                        hs = slice(h * HEAD, (h + 1) * HEAD)
                        dqt[hs, :] += nn(kvt_ref[hs, place], grad)
                    dva[place, :] += nn(jnp.concatenate(ps, axis=1), db)
                    dka[place, :] += nn(jnp.concatenate(ds, axis=1), qb)
                    return carry

                lax.fori_loop(0, patches // chunk, one_chunk, 0)

        dqc_ref[at, :] = (dqt[...] * SCALE).T.astype(BF)
        return carry

    lax.fori_loop(0, length // tile, one_tile, 0)
    dk_ref[...] = dka[...].astype(BF)
    dv_ref[...] = dva[...].astype(BF)


def call_cross_backward(plots, flags, tp, e2, gb, qc, qct, kv, kvt, ct, lse):
    width, length = qct.shape
    states = kv.shape[0]
    return pl.pallas_call(
        functools.partial(cross_backward_kernel, width // HEAD, plots),
        out_shape=[sds((length, width), BF), sds((states, width), BF), sds((states, width), BF)],
        in_specs=[SM] + [VM] * 9,
        out_specs=[VM] * 3,
        scratch_shapes=[
            pltpu.VMEM((states, width), F32),
            pltpu.VMEM((states, width), F32),
            pltpu.VMEM((width, 256), F32),
            pltpu.VMEM((states, width), BF),
        ],
        compiler_params=pltpu.CompilerParams(vmem_limit_bytes=VLIMIT),
        name="cross_backward",
    )(flags, tp, e2, gb, qc, qct, kv, kvt, ct, lse)


def self_backward_kernel(n, heads, plots, x0_ref, x1_ref, g2_ref, gain_ref, seg_ref, dqc_ref, dk_ref, dv_ref,
                         e2_hbm, h1_hbm, h0_hbm, ga_hbm, gb_hbm, m_hbm, c_hbm, a_hbm, qkv_hbm, qkvt_hbm, at_hbm, lse_hbm,
                         res_ref, mem_ref, dgain_ref, ga_grad_ref, gb_grad_ref,
                         e2, h1, h0, ga, gb, mem, c, a, qkv, qkvt, att, lse, e1, dqkv, dka, dva, tr, lsem, *rest):
    rest = list(rest)

    def take(count):
        got = rest[:count]
        del rest[:count]
        return got

    p = Place(n)
    tile, width_d = x1_ref.shape
    width = heads * HEAD
    length = e1.shape[0]
    tiles = length // tile
    loads = [
        pltpu.make_async_copy(s, d, lsem.at[i])
        for i, (s, d) in enumerate(
            ((ga_hbm, ga), (gb_hbm, gb), (m_hbm, mem), (h1_hbm, h1), (e2_hbm, e2), (c_hbm, c), (a_hbm, a),
             (qkv_hbm, qkv), (qkvt_hbm, qkvt), (at_hbm, att), (lse_hbm, lse), (h0_hbm, h0))
        )
    ]
    for load in loads:
        load.start()
    sums = [TensorSum(p, take(9)) for _ in range(2)]
    gather = TensorGather(p, e1, take(2), tile)
    ms0, ms1, mr0, mr1, mys, myr, mss, mrs = take(8)
    greet([p.core, p.y])
    loads[0].wait()
    wq = flat(ga)[:, 3 * width : 4 * width]
    sums[0].begin(lambda j: nt(dqc_ref[rows(j, tile), :], wq))
    loads[1].wait()

    patches = dk_ref.shape[0] // plots
    blocks = patches // 4 // 256

    def mem_rows(owner, b):
        plot, part = b // blocks, b % blocks
        return pl.ds(pl.multiple_of(plot * patches + owner * (patches // 4) + part * 256, 256), 256)

    def mem_part(owner, b):
        at = mem_rows(owner, b)
        return nt(dk_ref[at, :], flat(gb)[:, 0:width]) + nt(dv_ref[at, :], flat(gb)[:, width : 2 * width])

    total_blocks = plots * blocks
    mc0 = [rcopy(ms0.at[b], mr0.at[b], mss.at[0, b], mrs.at[0, b], p.core) for b in range(total_blocks)]
    mc1 = [rcopy(ms1.at[b], mr1.at[b], mss.at[1, b], mrs.at[1, b], p.core) for b in range(total_blocks)]
    mcy = [rcopy(mys.at[b], myr.at[b], mss.at[2, b], mrs.at[2, b], p.y) for b in range(total_blocks)]
    for b in range(total_blocks):
        ms0[b] = mem_part(p.tcy, b).astype(BF)
        mc0[b].start()
    for b in range(total_blocks):
        ms1[b] = mem_part(p.tc, b).astype(BF)
        mc1[b].start()

    dh1 = sums[0].end()
    x1 = x1_ref[...]
    dv1, dgain1 = norm_back(x1, gain_ref[1:2, :], dh1)
    dgain_ref[1:2, :] = dgain1
    g1 = g2_ref[...] + dv1
    gather.begin(g1.astype(BF))
    for b in range(total_blocks):
        mc0[b].wait_recv()
        mys[b] = (mem_part(p.ty, b) + mr0[b].astype(F32)).astype(BF)
        mcy[b].start()

    loads[2].wait()
    states = dk_ref.shape[0]
    for i in range(states // length):
        part = slice(i * length, (i + 1) * length)
        tr[...] = mem[part, :].T
        if i == 0:
            dka[...] = nn(tr[...], dk_ref[part, :])
            dva[...] = nn(tr[...], dv_ref[part, :])
        else:
            dka[...] += nn(tr[...], dk_ref[part, :])
            dva[...] += nn(tr[...], dv_ref[part, :])
    gb_grad_ref[:, 0:width] = dka[...].astype(BF)
    gb_grad_ref[:, width : 2 * width] = dva[...].astype(BF)
    loads[3].wait()
    tr[...] = h1[...].T
    ga_grad_ref[:, 3 * width : 4 * width] = nn(tr[...], dqc_ref[...]).astype(BF)
    loads[4].wait()
    loads[5].wait()
    tr[...] = e2[...].T
    gb_grad_ref[:, 3 * width : 4 * width] = nn(tr[...], c[...]).astype(BF)
    gather.forward()
    gather.end()

    for load in loads[6:]:
        load.wait()
    start = segment_starts(seg_ref[...])
    tr[...] = e1[...].T
    gb_grad_ref[:, 2 * width : 3 * width] = nn(tr[...], a[...]).astype(BF)
    wo = flat(gb)[:, 2 * width : 3 * width]
    for i in range(tiles):
        at = slice(i * tile, (i + 1) * tile)
        keys = (i + 1) * tile
        da = nn(e1[at, :], wo)
        dar = da.astype(BF)
        dat = da.T.astype(BF).astype(F32)
        qt = qkvt[0:width, at].astype(F32) * SCALE
        allowed = causal_mask(keys, tile, i, start[:, at])
        kk = qkv[0:keys, width : 2 * width]
        vv = qkv[0:keys, 2 * width : 3 * width]
        ps, ds, dq = [], [], []
        for h in range(heads):
            hs = slice(h * HEAD, (h + 1) * HEAD)
            inner = jnp.sum(dat[hs, :] * att[hs, at], axis=0, keepdims=True)
            prob = jnp.where(allowed, jnp.exp(nn(kk, head_rows(qt, h)) - lse[h : h + 1, at]), 0.0)
            grad = (prob * (nn(vv, head_rows(dat, h)) - inner)).astype(BF)
            ps.append(prob.astype(BF))
            ds.append(grad)
            dq.append(nn(qkvt[width + h * HEAD : width + (h + 1) * HEAD, 0:keys], grad))
        dqkv[at, 0:width] = (jnp.concatenate(dq, axis=0) * SCALE).T
        dk = nn(jnp.concatenate(ds, axis=1), head_block(qkv[at, 0:width].astype(F32) * SCALE, heads))
        dv = nn(jnp.concatenate(ps, axis=1), head_block(dar.astype(F32), heads))
        if i:
            dqkv[0 : keys - tile, width : 2 * width] += dk[0 : keys - tile]
            dqkv[0 : keys - tile, 2 * width : 3 * width] += dv[0 : keys - tile]
        dqkv[at, width : 2 * width] = dk[keys - tile :]
        dqkv[at, 2 * width : 3 * width] = dv[keys - tile :]
    sums[1].begin(lambda j: nt(dqkv[rows(j, tile), :].astype(BF), flat(ga)[:, 0 : 3 * width]))
    tr[...] = h0[...].T
    ga_grad_ref[:, 0 : 3 * width] = nn(tr[...], dqkv[...].astype(BF)).astype(BF)
    for b in range(total_blocks):
        mc1[b].wait_recv()
        mcy[b].wait_recv()
        own = mem_part(p.t, b) + mr1[b].astype(F32) + myr[b].astype(F32)
        mem_ref[b // blocks, (b % blocks) * 256 : (b % blocks + 1) * 256, :] = own.astype(BF)
    dh0 = sums[1].end()
    dv0, dgain0 = norm_back(x0_ref[...].astype(F32), gain_ref[0:1, :], dh0)
    dgain_ref[0:1, :] = dgain0
    res_ref[...] = (g1 + dv0).astype(BF)
    for group in (mc0, mc1, mcy):
        for cpy in group:
            cpy.wait_send()


def call_self_backward(n, plots, x0, x1, g2, gain, seg, dqc, dk, dv, e2, h1, h0, ga, gb, mem, c, a, qkv, qkvt, att, lse):
    tile, width_d = x1.shape
    length, width = dqc.shape
    states = mem.shape[0]
    patches = states // plots
    total_blocks = plots * (patches // 4 // 256)
    hbm = (e2, h1, h0, ga, gb, mem, c, a, qkv, qkvt, att, lse)
    scratch = [pltpu.VMEM(v.shape, v.dtype) for v in hbm]
    scratch += [
        pltpu.VMEM((length, width_d), BF),
        pltpu.VMEM((length, 3 * width), F32),
        pltpu.VMEM((width_d, width), F32),
        pltpu.VMEM((width_d, width), F32),
        pltpu.VMEM((width_d, length), BF),
        DMA((12,)),
    ]
    scratch += TensorSum.scratch(tile, width_d) * 2 + TensorGather.scratch()
    scratch += [pltpu.VMEM((total_blocks, 256, width_d), BF)] * 6 + [DMA((3, total_blocks))] * 2
    return pl.pallas_call(
        functools.partial(self_backward_kernel, n, width // HEAD, plots),
        out_shape=[
            sds((tile, width_d), BF),
            sds((plots, patches // 4, width_d), BF),
            sds((8, width_d), F32),
            sds((width_d, 4 * width), BF),
            sds((width_d, 4 * width), BF),
        ],
        in_specs=[VM] * 8 + [ANY] * 12,
        out_specs=[VM] * 5,
        scratch_shapes=scratch,
        compiler_params=pltpu.CompilerParams(collective_id=3, has_side_effects=True, vmem_limit_bytes=VLIMIT),
        name="self_backward",
    )(x0, x1, g2, gain, seg, dqc, dk, dv, *hbm)


class RowSum:
    def __init__(self, place, mine, near, mid, far, sems):
        self.p = place
        self.mine, self.near, self.mid, self.far = mine, near, mid, far
        self.xs, self.xr, self.zs, self.zr = sems
        self.steps = place.n // 2

    @staticmethod
    def scratch(n, shard, width):
        half = (n // 2, shard, width)
        return [pltpu.VMEM(half, BF)] * 3 + [DMA((n // 2,))] * 4

    def slot(self, k):
        return lax.rem(self.p.d + 2 * k, self.p.n)

    def xcopy(self, k):
        return rcopy(self.mine.at[lax.rem(self.p.dx + 2 * k, self.p.n)], self.near.at[k], self.xs.at[k], self.xr.at[k], self.p.x)

    def zcopy(self, k):
        return rcopy(self.mid.at[k], self.far.at[k], self.zs.at[k], self.zr.at[k], self.p.z(k))

    def begin(self):
        for k in list(range(1, self.steps)) + [0]:
            self.xcopy(k).start()

    def middle(self):
        for k in range(1, self.steps):
            self.xcopy(k).wait_recv()
            self.mid[k] = (self.mine[self.slot(k)].astype(F32) + self.near[k].astype(F32)).astype(BF)
            self.zcopy(k).start()

    def end(self):
        self.xcopy(0).wait_recv()
        total = self.mine[self.p.d].astype(F32) + self.near[0].astype(F32)
        for k in range(1, self.steps):
            self.zcopy(k).wait_recv()
            total = total + self.far[k].astype(F32)
        return total

    def sent(self):
        for k in range(1, self.steps):
            self.zcopy(k).wait_send()
        for k in range(self.steps):
            self.xcopy(k).wait_send()


def grads_kernel(n, du_ref, gb_ref, ga_ref, dgain_ref, du_out, gb_out, ga_out, stat_ref,
                 stat_t, stat_d, tsem_s, tsem_r, dsem_s, dsem_r, *rest):
    rest = list(rest)

    def take(count):
        got = rest[:count]
        del rest[:count]
        return got

    p = Place(n)
    grads = (du_ref, gb_ref, ga_ref)
    outs = (du_out, gb_out, ga_out)
    sums = []
    for g in grads:
        near, mid, far, xs, xr, zs, zr = take(7)
        sums.append(RowSum(p, g, near, mid, far, (xs, xr, zs, zr)))
    tensor_peers = [(p.d, lax.rem(p.t + k, 4)) for k in range(1, 4)]
    dp_peers = [(lax.rem(p.d + k, n), p.t) for k in range(1, n)]
    greet(tensor_peers + dp_peers)
    for s in sums:
        s.begin()
    for s in sums:
        s.middle()
    squares = jnp.zeros((1, 1), F32)
    for s, o in zip(sums, outs):
        total = s.end()
        o[...] = total
        squares = squares + jnp.sum(jnp.sum(total * total, axis=1, keepdims=True), axis=0, keepdims=True)
    row = lax.broadcasted_iota(jnp.int32, dgain_ref.shape, 0)
    stat_t[0] = jnp.where(row < 3, dgain_ref[...], jnp.where(row == 3, squares, 0.0))
    copies = [rcopy(stat_t.at[0], stat_t.at[k], tsem_s.at[k], tsem_r.at[k], tensor_peers[k - 1]) for k in range(1, 4)]
    for c in copies:
        c.start()
    for c in copies:
        c.wait_recv()
    total = jnp.zeros(dgain_ref.shape, F32)
    for j in range(4):
        total = total + stat_t[lax.rem(p.t - j + 4, 4)]
    stat_d[0] = total
    copies2 = [rcopy(stat_d.at[0], stat_d.at[k], dsem_s.at[k], dsem_r.at[k], dp_peers[k - 1]) for k in range(1, n)]
    for c in copies2:
        c.start()
    for c in copies2:
        c.wait_recv()
    total = jnp.zeros(dgain_ref.shape, F32)
    for j in range(n):
        total = total + stat_d[lax.rem(p.d - j + n, n)]
    stat_ref[...] = total
    for c in copies + copies2:
        c.wait_send()
    for s in sums:
        s.sent()


def call_grads(n, du, gb, ga, dgain):
    width_d = dgain.shape[1]
    shard = width_d // n
    grads = [g.reshape(n, shard, g.shape[1]) for g in (du, gb, ga)]
    scratch = [
        pltpu.VMEM((4, 8, width_d), F32),
        pltpu.VMEM((n, 8, width_d), F32),
        DMA((4,)),
        DMA((4,)),
        DMA((n,)),
        DMA((n,)),
    ]
    for g in grads:
        scratch += RowSum.scratch(n, shard, g.shape[2])
    return pl.pallas_call(
        functools.partial(grads_kernel, n),
        out_shape=[sds((shard, g.shape[2]), F32) for g in grads] + [sds((8, width_d), F32)],
        in_specs=[VM] * 4,
        out_specs=[VM] * 4,
        scratch_shapes=scratch,
        compiler_params=pltpu.CompilerParams(collective_id=4, has_side_effects=True, vmem_limit_bytes=VLIMIT),
        name="grads",
    )(*grads, dgain)


def adam_step(master, moment, second, gradient, step_rate, decay_rate):
    moment_new = BETA_ONE * moment + (1.0 - BETA_ONE) * gradient
    second_new = BETA_TWO * second + (1.0 - BETA_TWO) * gradient * gradient
    moment_hat = moment_new / (1.0 - BETA_ONE**STEP)
    second_hat = second_new / (1.0 - BETA_TWO**STEP)
    master_new = master - step_rate * (
        moment_hat / (jnp.sqrt(second_hat) + ADAM_EPS) + decay_rate * master
    )
    return (master_new, moment_new, second_new)


def local(
    n,
    residual,
    cotangent,
    memory,
    segment_ids,
    plot_ids,
    attend_weight,
    attend_first,
    attend_second,
    recall_weight,
    recall_first,
    recall_second,
    outward_weight,
    outward_first,
    outward_second,
    expand_weight,
    expand_first,
    expand_second,
    narrow_weight,
    narrow_first,
    narrow_second,
    gain_weight,
    gain_first,
    gain_second,
):
    _, plots, patches, width_d = memory.shape
    shard = attend_weight.shape[1]
    aligned = shard % 16 == 0
    length = segment_ids.shape[1]

    def by_rows(w):
        return jnp.transpose(w, (1, 0, 2)).reshape(w.shape[1], -1)

    sa = by_rows(attend_weight).astype(BF)
    sb = jnp.concatenate(
        [by_rows(recall_weight), by_rows(jnp.transpose(outward_weight, (0, 2, 1)))], axis=1
    ).astype(BF)
    sc = jnp.concatenate([by_rows(expand_weight), narrow_weight.T], axis=1).astype(BF)
    if not aligned:
        sa, sb, sc = (
            lax.all_gather(s, "dp", axis=0, tiled=True).reshape(8, width_d // 8, s.shape[1]) for s in (sa, sb, sc)
        )
    mem = memory.reshape(plots * patches, width_d)
    token_plots = jnp.sum(
        jnp.where(segment_ids[:, :, None] == jnp.arange(SEGS)[None, None, :], plot_ids[:, None, :], 0), axis=-1
    )
    flags = (
        jnp.any(token_plots.reshape(length // 256, 1, 256) == jnp.arange(plots)[None, :, None], axis=-1)
        .astype(jnp.int32)
        .reshape(-1)
    )
    x0 = residual[0]
    qkv, qkvt, a, att, lse, x1, qc, qct, ga, gb, gc, h0, h1, e3, kv, kvt = call_first(
        n, aligned, x0, cotangent[0], gain_weight, segment_ids, sa, sb, sc, mem
    )
    ct, c, lse_c = call_cross_forward(plots, flags, token_plots, qct, kv, kvt)
    x2, block_out, g2, e2, dgain2, du = call_ffn(n, c, x1, gain_weight, gb, gc, e3)
    dqc, dk, dv = call_cross_backward(plots, flags, token_plots, e2, gb, qc, qct, kv, kvt, ct, lse_c)
    residual_grad, memory_grad, dgain, dga, dgb = call_self_backward(
        n, plots, x0, x1, g2, gain_weight, segment_ids, dqc, dk, dv, e2, h1, h0, ga, gb, mem, c, a, qkv, qkvt, att, lse
    )
    dgain = jnp.concatenate([dgain[0:2], dgain2, jnp.zeros((5, width_d), F32)], axis=0)
    if aligned:
        own_u, own_b, own_a, stat = call_grads(n, du, dgb, dga, dgain)
        square_total = stat[3, 0]
        gain_total = stat[0:3]
    else:
        own_u, own_b, own_a = (
            lax.psum_scatter(g.astype(F32), "dp", scatter_dimension=0, tiled=True) for g in (du, dgb, dga)
        )
        squares = sum(jnp.sum(g * g) for g in (own_u, own_b, own_a))
        gain_total, square_total = lax.psum((dgain[0:3], squares), ("dp", "tensor"))
    grad_norm = jnp.sqrt(square_total + jnp.sum(gain_total * gain_total))
    factor = jnp.minimum(1.0, CLIP / (grad_norm + 1e-06))

    width = attend_weight.shape[2]
    hidden = expand_weight.shape[2]
    grads = (
        jnp.stack([own_a[:, i * width : (i + 1) * width] for i in range(4)]),
        jnp.stack([own_b[:, i * width : (i + 1) * width] for i in range(2)]),
        jnp.stack([own_b[:, i * width : (i + 1) * width].T for i in (2, 3)]),
        jnp.stack([own_u[:, i * hidden : (i + 1) * hidden] for i in range(2)]),
        own_u[:, 2 * hidden :].T,
    )
    masters = (attend_weight, recall_weight, outward_weight, expand_weight, narrow_weight)
    moments = (attend_first, recall_first, outward_first, expand_first, narrow_first)
    seconds = (attend_second, recall_second, outward_second, expand_second, narrow_second)
    step_rates = (RATE_INNER, RATE_INNER, RATE_OUTER, RATE_INNER, RATE_INNER)
    results = []
    for master, moment, second, gradient, step_rate in zip(masters, moments, seconds, grads, step_rates):
        master_new, moment_new, second_new = adam_step(
            master, moment, second, gradient * factor, step_rate, DECAY
        )
        results.extend([master_new, moment_new, second_new, master_new.astype(BF)])
    gain_new = adam_step(gain_weight, gain_first, gain_second, gain_total * factor, RATE_GAIN, 0.0)
    return (
        (block_out[None], residual_grad[None], memory_grad[None], grad_norm) + tuple(results) + tuple(gain_new)
    )


def solution(mesh):
    rows_in = P("dp", "tensor", None)
    inner = P(None, "dp", "tensor")
    outer = P(None, "tensor", "dp")
    narrow = P("tensor", "dp")
    in_specs = (
        (rows_in, rows_in, P("dp", None, None, None), P("dp", None), P("dp", None))
        + (inner,) * 3
        + (inner,) * 3
        + (outer,) * 3
        + (inner,) * 3
        + (narrow,) * 3
        + (P(),) * 3
    )
    out_specs = (
        (rows_in, rows_in, P("dp", None, "tensor", None), P())
        + (inner,) * 4
        + (inner,) * 4
        + (outer,) * 4
        + (inner,) * 4
        + (narrow,) * 4
        + (P(),) * 3
    )
    return jax.shard_map(
        functools.partial(local, mesh.shape["dp"]),
        mesh=mesh,
        in_specs=in_specs,
        out_specs=out_specs,
        check_vma=False,
    )
```

time: 1120 us -> 401 us (0.36); the launches traced: 1110 us -> 403 us
  waiting for transfers between devices: 522 us -> 0 us
  Pallas kernels: 0 us -> 375 us
  matrix products: 260 us -> 0 us
  blocking collectives: 140 us -> 0 us
  other arithmetic: 112 us -> 12.7 us
  local copies, waits for them, and re-layouts: 50.7 us -> 11.3 us
  between operations: 22.1 us -> 3.77 us
    pallas_call x0 -> x6, Pallas kernels: none -> 375 us  [the longest x1 87.1 us: call_grads(): pl.pallas_call(functools.partial(grads_kernel, n), out_shape=[sds((shard,...]
    dot_general x61 -> x0, matrix products: 260 us -> none  [the longest x4 43.1 us: attend_backward(): jnp.einsum('rqhd,rkhd->rhqk', grad_block, values_all, preferred_element_t...]
    reduce_scatter x9 -> x0, waiting for transfers between devices: 226 us -> none  [the longest x3 114 us: sum_branch(): lax.psum_scatter(partial_out, 'tensor', scatter_dimension=1, tiled=True)]
    unnamed x23 -> x0, waiting for transfers between devices: 199 us -> none
    all_gather x3 -> x0, blocking collectives: 101 us -> none  [the longest x1 35.3 us: local(): lax.all_gather(outward_weight.astype(jnp.bfloat16), 'dp', axis=2, tiled=T...]
    all_gather x8 -> x0, waiting for transfers between devices: 96.8 us -> none  [the longest x3 42.6 us: spread_rows(): return lax.all_gather(normed, 'tensor', axis=1, tiled=True)]
    convert_element_type x19 -> x7, other arithmetic: 61.7 us -> 5.56 us  [the longest x5 5.53 us: local(): results.extend([master_new, moment_new, second_new, master_new.astype(BF)])]
    unnamed x255 -> x66, local copies, waits for them, and re-layouts: 47.5 us -> 6.91 us
  transfers between devices with their start and end apart: 20 -> 0, of which waited for: 16 -> 0; matrix products, arithmetic and copies ran while one was open for 19% -> 0% of each run, Pallas kernels for 0% -> 0%
where the time goes in v1:
time: 401 us; the launch traced here: 403 us
  Pallas kernels  375 us (94%)
  other arithmetic  12.7 us (3%)
  local copies, waits for them, and re-layouts  11.3 us (3%)
    pallas_call x1, Pallas kernels, call_grads(): pl.pallas_call(functools.partial(grads_kernel, n), out_shape=[sds((shard,...  87.1 us
    pallas_call x1, Pallas kernels, call_first(): pl.pallas_call(functools.partial(first_kernel, n, gather, heads), out_sha...  81.9 us
    pallas_call x1, Pallas kernels, call_self_backward(): pl.pallas_call(functools.partial(self_backward_kernel, n, width // HEAD,...  73.2 us
    pallas_call x1, Pallas kernels, call_ffn(): pl.pallas_call(functools.partial(ffn_kernel, n, width // HEAD), out_shape...  64.8 us
    pallas_call x1, Pallas kernels, call_cross_backward(): pl.pallas_call(functools.partial(cross_backward_kernel, width // HEAD, pl...  38.6 us
    pallas_call x1, Pallas kernels, call_cross_forward(): pl.pallas_call(functools.partial(cross_forward_kernel, heads, plots), out...  29.5 us

profile of v1, /device:TPU:0, one launch (start us, length us, event | category | flops | bytes accessed | tf_op | source)
XLA Modules:
  0.0 402.8 jit_solution(17016197954699975198)
XLA Ops:
  0.7 0.0 copy-start.5
  0.7 0.0 copy-start.3
  0.7 0.0 copy-start.2
  0.7 1.1 convert_bitcast_fusion
  1.8 0.9 convert_bitcast_fusion.2
  2.8 0.7 pad_maximum_fusion.sc_ref
  3.5 0.0 copy-done.5
  3.5 0.1 copy.76
  3.6 0.1 reshape.158
  3.7 0.0 copy-done.3
  3.8 0.1 copy.87
  3.9 0.7 pad_maximum_fusion.1.sb_ref
  4.6 0.0 copy-done.2
  4.6 0.2 copy.75
  4.8 0.9 convert_element_type.35.sa_ref
  5.6 81.9 %self_forward.1 = (bf16[1024,576]{1,0:T(8,128)(2,1)}, bf16[576,1024]{1,0:T(8,128)(2,1)}, bf16[1024,192]{1,0:T(8,128)(2,1)}, f32[192,1024]{1,0:T(8,128)}, f32[8,1...) custom-call(bf16[256,768]{1,0:T(8,128)(2,1)} %bitcast.61, ...), custom_call_target="tpu_custom_call" | custom-call | tf_op jit(solution)/shard_map/self_forward/pallas_call | solution.py:416
  87.5 0.0 copy-done.23
  87.5 0.1 select_reduce_fusion
  87.6 0.0 copy-start.22
  87.6 0.1 fusion.7
  87.8 0.1 copy.74
  87.9 0.6 reshape.165.flags_ref
  88.5 0.0 copy-done.22
  88.5 29.5 %cross_forward.1 = (f32[192,1024]{1,0:T(8,128)}, bf16[1024,192]{1,0:T(8,128)(2,1)}, f32[8,1024]{1,0:T(8,128)}) custom-call(s32[8]{0:T(128)} %reshape.165.flags_ref, s32[1,1024]{1,0:T(1,128)} %bitcast.70, bf16[192,1024]{1,0:T(8,128)(2,1)} %get-tuple-element.63.qct_ref, bf16[4096,384]{1,0:T(8,128)(2,1)} %get-tuple-element.64.kv_ref, ...), custom_call_target="tpu_custom_call" | custom-call | tf_op jit(solution)/shard_map/cross_forward/pallas_call | solution.py:482
  118.0 64.8 %ffn.1 = (f32[256,768]{1,0:T(8,128)}, bf16[256,768]{1,0:T(8,128)(2,1)}, f32[256,768]{1,0:T(8,128)}, bf16[1024,768]{1,0:T(8,128)(2,1)}, f32[1,768]{1,0:T(1,128)}, /*index=5*/bf16[768,1536]{1,0:T(8,128)(2,1)}) custom-call(bf16[1024,192]{1,0:T(8,128)(2,1)} %get-tuple-element.66.c_ref.c_hbm, f32[256,768]{1,0:T(8,128)} %get-tuple-element.67.x1_ref, ...), custom_call_target="tpu_custom_call" | custom-call | tf_op jit(solution)/shard_map/ffn/pallas_call | solution.py:573
  182.8 38.6 %cross_backward.1 = (bf16[1024,192]{1,0:T(8,128)(2,1)}, bf16[4096,192]{1,0:T(8,128)(2,1)}, bf16[4096,192]{1,0:T(8,128)(2,1)}) custom-call(s32[8]{0:T(128)} %reshape.165.flags_ref, s32[1,1024]{1,0:T(1,128)} %bitcast.71, bf16[1024,768]{1,0:T(8,128)(2,1)} %get-tuple-element.73.e2_ref.e2_hbm, bf16[8,96,768]{2,1,0:T(8,128)(2,1)} %get-tuple-element.68.gb_ref.gb_hbm, ...), custom_call_target="tpu_custom_call" | custom-call | tf_op jit(solution)/shard_map/cross_backward/pallas_call | solution.py:654
  221.4 73.2 %self_backward.1 = (bf16[256,768]{1,0:T(8,128)(2,1)}, bf16[2,512,768]{2,1,0:T(8,128)(2,1)}, f32[8,768]{1,0:T(8,128)}, bf16[768,768]{1,0:T(8,128)(2,1)}, bf16[768,768]{1,0:T(8,128)(2,1)}) custom-call(bf16[256,768]{1,0:T(8,128)(2,1)} %bitcast.62, f32[256,768]{1,0:T(8,128)} %get-tuple-element.67.x1_ref, f32[256,768]{1,0:T(8,128)} %get-tuple-element.72.g2_ref, ...), custom_call_target="tpu_custom_call" | custom-call | tf_op jit(solution)/shard_map/self_backward/pallas_call | solution.py:828
  294.6 0.7 slice.42
  295.4 0.1 pad.12.clone
  295.4 0.7 maximum_maximum_fusion.dgain_ref
  296.1 0.0 copy-start.17
  296.1 0.0 copy-start.18
  296.1 87.1 %grads.1 = (f32[96,1536]{1,0:T(8,128)}, f32[96,768]{1,0:T(8,128)}, f32[96,768]{1,0:T(8,128)}, f32[8,768]{1,0:T(8,128)}) custom-call(bf16[8,96,1536]{2,1,0:T(8,128)(2,1)} %bitcast.59, bf16[8,96,768]{2,1,0:T(8,128)(2,1)} %bitcast.64, bf16[8,96,768]{2,1,0:T(8,128)(2,1)} %bitcast.63, f32[8,768]{1,0:T(8,128)} %maximum_maximum_fusion.dgain_ref), custom_call_target="tpu_custom_call" | custom-call | tf_op jit(solution)/shard_map/grads/pallas_call | solution.py:959
  383.2 0.0 copy-start.1
  383.2 0.0 copy-start.9
  383.3 0.0 copy-start.10
  383.3 1.3 slice.43
  384.6 1.3 multiply_reduce_fusion
  387.3 1.4 multiply_subtract_fusion.5
  388.7 0.0 copy-done.17
  388.7 1.9 fusion.9
  390.6 0.0 copy-done.6
  390.7 0.0 copy-start.15
  390.7 1.3 fusion.12
  392.0 0.2 slice_bitcast_fusion.3
  392.2 0.1 copy.79
  392.3 0.6 copy-done.16
  392.9 0.1 copy.80
  393.0 0.0 copy-start.19
  393.0 0.0 copy-start.20
  393.0 0.1 copy.82
  393.2 0.2 fusion.14
  393.4 0.0 copy-start.11
  393.4 0.0 copy-start.12
  393.4 0.8 copy.83
  394.2 0.8 copy.84
  395.0 0.8 copy.85
  395.8 0.7 copy.86
  396.6 0.0 copy-done.19
  396.6 0.9 fusion.16
  397.5 1.3 fusion.18
  398.8 0.7 copy.92
  399.6 0.7 copy.93
  400.3 1.1 copy.94
  (41 shorter events, 0.2 us)
Async XLA Ops:
  0.7 2.8 copy-start.5
  0.7 3.1 copy-start.3
  0.7 3.9 copy-start.2
  5.6 81.9 %copy-start.23 = (s32[1,1024]{1,0:T(1,128)S(1)}, s32[1,1024]{1,0:T(1,128)}, u32[]{:S(2)}) copy-start(s32[1,1024]{1,0:T(1,128)} %seg_ref.3) | copy-start | bytes 12292
  5.6 81.9 %copy-start.27 = (s32[1,4]{1,0:T(1,128)S(1)}, s32[1,4]{1,0:T(1,128)}, u32[]{:S(2)}) copy-start(s32[1,4]{1,0:T(1,128)} %param.27) | copy-start | bytes 52
  87.6 0.9 copy-start.22
  221.4 74.0 %copy-start.26 = (f32[1,768]{1,0:T(1,128)S(1)}, f32[1,768]{1,0:T(1,128)}, u32[]{:S(2)}) copy-start(f32[1,768]{1,0:T(1,128)} %get-tuple-element.94) | copy-start | bytes 9220
  296.1 91.2 %copy-start.21 = (f32[3,768]{1,0:T(4,128)S(1)}, f32[3,768]{1,0:T(4,128)}, u32[]{:S(2)}) copy-start(f32[3,768]{1,0:T(4,128)} %gain_ref.5) | copy-start | bytes 27652
  296.1 91.2 %copy-start.24 = (f32[3,768]{1,0:T(4,128)S(1)}, f32[3,768]{1,0:T(4,128)}, u32[]{:S(2)}) copy-start(f32[3,768]{1,0:T(4,128)} %param.44) | copy-start | bytes 27652
  296.1 91.2 %copy-start.25 = (f32[3,768]{1,0:T(4,128)S(1)}, f32[3,768]{1,0:T(4,128)}, u32[]{:S(2)}) copy-start(f32[3,768]{1,0:T(4,128)} %param.45) | copy-start | bytes 27652
  296.1 92.6 %copy-start.4 = (f32[512,96]{0,1:T(8,128)S(1)}, f32[512,96]{0,1:T(8,128)}, u32[]{:S(2)}) copy-start(f32[512,96]{0,1:T(8,128)} %param.40) | copy-start | bytes 589828
  296.1 92.6 %copy-start.17 = (f32[512,96]{0,1:T(8,128)S(1)}, f32[512,96]{0,1:T(8,128)}, u32[]{:S(2)}) copy-start(f32[512,96]{0,1:T(8,128)} %param.41) | copy-start | bytes 589828
  296.1 92.6 %copy-start.18 = (f32[512,96]{0,1:T(8,128)S(1)}, f32[512,96]{0,1:T(8,128)}, u32[]{:S(2)}) copy-start(f32[512,96]{0,1:T(8,128)} %param.42) | copy-start | bytes 589828
  383.2 7.4 %copy-start.6 = (f32[96,1536]{1,0:T(8,128)S(1)}, f32[96,1536]{1,0:T(8,128)}, u32[]{:S(2)}) copy-start(f32[96,1536]{1,0:T(8,128)} %get-tuple-element.98) | copy-start | bytes 1769476
  383.2 7.4 %copy-start.1 = (f32[2,96,512]{2,1,0:T(8,128)S(1)}, f32[2,96,512]{2,1,0:T(8,128)}, u32[]{:S(2)}) copy-start(f32[2,96,512]{2,1,0:T(8,128)} %param.37) | copy-start | bytes 1179652
  383.2 7.4 %copy-start.9 = (f32[2,96,512]{2,1,0:T(8,128)S(1)}, f32[2,96,512]{2,1,0:T(8,128)}, u32[]{:S(2)}) copy-start(f32[2,96,512]{2,1,0:T(8,128)} %param.38) | copy-start | bytes 1179652
  383.3 7.4 %copy-start.10 = (f32[2,96,512]{2,1,0:T(8,128)S(1)}, f32[2,96,512]{2,1,0:T(8,128)}, u32[]{:S(2)}) copy-start(f32[2,96,512]{2,1,0:T(8,128)} %param.39) | copy-start | bytes 1179652
  390.6 1.4 copy-start.7
  390.6 1.3 copy-start.8
  390.7 1.5 copy-start.15
  392.0 0.9 copy-start.16
  393.0 3.5 copy-start.19
  393.0 3.5 copy-start.20
  393.4 4.1 %copy-start.11 = (f32[4,96,192]{2,1,0:T(8,128)S(1)}, f32[4,96,192]{2,1,0:T(8,128)}, u32[]{:S(2)}) copy-start(f32[4,96,192]{2,1,0:T(8,128)} %param.29) | copy-start | bytes 884740
  393.4 4.1 %copy-start.12 = (f32[4,96,192]{2,1,0:T(8,128)S(1)}, f32[4,96,192]{2,1,0:T(8,128)}, u32[]{:S(2)}) copy-start(f32[4,96,192]{2,1,0:T(8,128)} %param.30) | copy-start | bytes 884740
  397.5 1.3 copy-start.13
  397.5 2.0 copy-start.14
  397.5 2.8 copy-start
